TPU v7x, 256 devices: a whole 4x4x8 slice. The times are simulated.
256 devices in a mesh: gx: 8 (over x, core), gy: 32 (over y, z).
Axes of the slice: x: 4, y: 4, z: 8, core: 2. Of those that a mesh axis runs over, the one named last changes fastest.
Arguments:
- span: float32 [524288, 256], P(('gx', 'gy')), as said below
- prior: float32 [256, 256], replicated, as said below
- counts: int32 [256], P(('gx', 'gy')), may hold values from 128 to 2048, as said below
Outputs:
- r_scaled: float32 [256, 256], replicated
- q_scaled: float32 [524288, 256], P(('gx', 'gy'))
Inputs may be any that keep to these rules, and one draw needn't show every extreme that they name: counts[d] is the number of live rows at the start of device block d; at least one block is full. prior is upper triangular with a positive diagonal. `span`: rows that are not live hold arbitrary values.
All inputs are finite; a program needn't handle non-finite values.
Results may differ from a plain program's by a relative error of at most 0.0003.
Values sent between devices are 32-bit elements; how exact they have to be, the bound alone decides.
No kernel may reach another device: no remote copies, remote signals or barrier semaphores. Data moves between devices by JAX's collectives and lax.ppermute only.
A program may use at most 64 MiB of HBM per device.

v0:
```python
import math

import jax
import jax.numpy as jnp
from jax import lax
from jax.sharding import PartitionSpec as P

exact_mode = lax.Precision.HIGHEST


def gram_of(rows_in):
    return lax.dot_general(
        rows_in,
        rows_in,
        (((0,), (0,)), ((), ())),
        precision=exact_mode,
        preferred_element_type=jnp.float32,
    )


def cholesky_lower(gram_mat):
    size_n = gram_mat.shape[0]
    row_ids = jnp.arange(size_n)

    def column_step(col, lower):
        target = lax.dynamic_slice_in_dim(gram_mat, col, 1, 1)[:, 0]
        lower_row = lax.dynamic_slice_in_dim(lower, col, 1, 0)[0]
        vector = target - jnp.dot(
            lower, lower_row, precision=exact_mode, preferred_element_type=jnp.float32
        )
        pivot = jnp.sqrt(lax.dynamic_slice_in_dim(vector, col, 1, 0)[0])
        column = jnp.where(row_ids >= col, vector / pivot, 0.0)
        return lax.dynamic_update_slice_in_dim(lower, column[:, None], col, 1)

    return lax.fori_loop(0, size_n, column_step, jnp.zeros_like(gram_mat))


def upper_inverse(r_upper):
    size_n = r_upper.shape[0]
    col_ids = jnp.arange(size_n)

    def row_step(turn, inverse):
        row = size_n - 1 - turn
        r_row = lax.dynamic_slice_in_dim(r_upper, row, 1, 0)[0]
        pivot = lax.dynamic_slice_in_dim(r_row, row, 1, 0)[0]
        beyond = jnp.where(col_ids > row, r_row, 0.0)
        unit = (col_ids == row).astype(jnp.float32)
        new_row = (
            unit
            - jnp.dot(beyond, inverse, precision=exact_mode, preferred_element_type=jnp.float32)
        ) / pivot
        return lax.dynamic_update_slice_in_dim(inverse, new_row[None, :], row, 0)

    return lax.fori_loop(0, size_n, row_step, jnp.zeros_like(r_upper))


def factor_rows(rows_in, live_rows, prior, row_scale):
    row_count, col_count = rows_in.shape
    block_rows = min(512, row_count)
    block_count = (live_rows + block_rows - 1) // block_rows
    prior_inverse = upper_inverse(prior)
    identity = jnp.eye(col_count, dtype=jnp.float32)

    def first_step(step, carry):
        accum, y_rows = carry
        row_start = step * block_rows
        row_block = lax.dynamic_slice_in_dim(rows_in, row_start, block_rows, 0)
        keep_rows = (row_start + jnp.arange(block_rows) < live_rows)[:, None]
        row_block = jnp.where(keep_rows, row_block, 0.0)
        image_rows = jnp.dot(
            row_block, prior_inverse, precision=exact_mode, preferred_element_type=jnp.float32
        )
        y_rows = lax.dynamic_update_slice_in_dim(y_rows, image_rows, row_start, 0)
        return (accum + gram_of(image_rows), y_rows)

    gram_one, y_rows = lax.fori_loop(
        0,
        block_count,
        first_step,
        (
            jnp.zeros((col_count, col_count), jnp.float32),
            jnp.zeros((row_count, col_count), jnp.float32),
        ),
    )
    gram_one = lax.psum(gram_one, ("gx", "gy"))
    gram_one = gram_one + identity
    upper_two = cholesky_lower(gram_one).T
    inverse_two = upper_inverse(upper_two)
    r_factor = jnp.dot(upper_two, prior, precision=exact_mode, preferred_element_type=jnp.float32)

    def basis_step(step, q_basis):
        row_start = step * block_rows
        row_block = lax.dynamic_slice_in_dim(y_rows, row_start, block_rows, 0)
        q_block = (
            jnp.dot(
                row_block, inverse_two, precision=exact_mode, preferred_element_type=jnp.float32
            )
            * row_scale
        )
        return lax.dynamic_update_slice_in_dim(q_basis, q_block, row_start, 0)

    q_basis = lax.fori_loop(
        0, block_count, basis_step, jnp.zeros((row_count, col_count), jnp.float32)
    )
    return (r_factor / row_scale, q_basis)


def per_device(span, prior, counts):
    row_count, col_count = span.shape
    all_rows = row_count * lax.axis_size("gx") * lax.axis_size("gy")
    row_scale = math.sqrt(all_rows)
    r_scaled, q_scaled = factor_rows(span, counts[0], prior, row_scale)
    return (r_scaled, q_scaled)


def solution(mesh):
    in_specs = (P(("gx", "gy"), None), P(), P(("gx", "gy")))
    out_specs = (P(), P(("gx", "gy"), None))
    return jax.shard_map(
        per_device, mesh=mesh, in_specs=in_specs, out_specs=out_specs, check_vma=False
    )
```

profile of v0, /device:TPU:1, one launch (start us, length us, event | category | flops | bytes accessed | tf_op | source)
XLA Modules:
  0.0 2060.7 jit_solution(16959032822959239776)
XLA Ops:
  7.9 752.9 %while.75 = (s32[]{:T(128)}, f32[256,256]{1,0:T(8,128)S(1)}, f32[256,256]{1,0:T(8,128)}, s32[]{:T(128)}, s32[]{:T(128)}, /*index=5*/s32[]{:T(128)}, s32[]{:T(128)}) while((s32[]{:T(128)}, f32[256,256]{1,0:T(8,128)S(1)}, f32[256,256]{1,0:T(8,128)}, s32[]{:T(128)}, s32[]{:T(128)}, /*index=5*/s32[]{:T(128)}, ...), condition=%wide.region_1.2_spmd.clone.clone, body=%wide.region_0.1_spmd.clone.clone.sunk | while | flops 787975 | bytes 272563 | solution.py:54
  13.8 1.3 dynamic_slice.100
  19.7 1.3 dynamic_slice.100
  22.6 1.3 dynamic_slice.100
  28.5 1.3 dynamic_slice.100
  37.3 1.3 dynamic_slice.100
  46.2 1.3 dynamic_slice.100
  52.0 1.3 dynamic_slice.100
  55.0 1.3 dynamic_slice.100
  60.9 1.3 dynamic_slice.100
  69.7 1.3 dynamic_slice.100
  75.6 1.3 dynamic_slice.100
  78.5 1.3 dynamic_slice.100
  84.4 1.3 dynamic_slice.100
  93.2 1.3 dynamic_slice.100
  102.0 1.3 dynamic_slice.100
  107.9 1.3 dynamic_slice.100
  110.9 1.3 dynamic_slice.100
  116.7 1.3 dynamic_slice.100
  125.6 1.3 dynamic_slice.100
  131.4 1.3 dynamic_slice.100
  761.0 6.9 while.72
  761.7 1.7 constant_dynamic-update-slice_fusion.2
  765.1 1.7 constant_dynamic-update-slice_fusion.2
  768.7 259.1 %all-reduce.2.cloned.1.call-done = f32[256,256]{0,1:T(8,128)} async-done(((f32[256,256]{0,1:T(8,128)}), f32[256,256]{0,1:T(8,128)}) %all-reduce.2.cloned.1.call-update) | async-done | bytes 262160 | tf_op jit(solution)/shard_map/psum | solution.py:85
  1028.9 619.7 %while.74 = (s32[]{:T(128)}, f32[256,256]{1,0:T(8,128)S(1)}, f32[256,256]{0,1:T(8,128)S(1)}, s32[]{:T(128)}, s32[]{:T(128)}) while((s32[]{:T(128)}, f32[256,256]{1,0:T(8,128)S(1)}, f32[256,256]{0,1:T(8,128)S(1)}, s32[]{:T(128)}, s32[]{:T(128)}) %tuple.151), condition=%wide.region_6.7_spmd.clone, body=%wide.region_5.6_spmd.clone.sunk | while | flops 787458 | bytes 275565 | solution.py:35
  1648.7 1.3 convolution_multiply_fusion.1
  1650.0 399.6 %while.76 = (s32[]{:T(128)}, f32[256,256]{1,0:T(8,128)S(1)}, f32[256,256]{1,0:T(8,128)S(1)}, s32[]{:T(128)}, s32[]{:T(128)}, /*index=5*/s32[]{:T(128)}, s32[]{:T(128)}) while((s32[]{:T(128)}, f32[256,256]{1,0:T(8,128)S(1)}, f32[256,256]{1,0:T(8,128)S(1)}, s32[]{:T(128)}, s32[]{:T(128)}, /*index=5*/s32[]{:T(128)}, ...), condition=%wide.region_8.9_spmd.clone.clone, body=%wide.region_7.8_spmd.clone.clone.sunk | while | flops 787975 | bytes 272563 | solution.py:54
  2049.7 1.5 broadcast.20
  2051.1 2.8 while.73
  2051.1 1.4 fusion.59
  2052.5 1.4 fusion.59
  (4860 shorter events, 1543.1 us)
Async XLA Ops:
  7.2 1020.7 %all-reduce.2.cloned.1.call-start = ((), (), s32[]{:S(2)}) async-start(), calls=%async_computation | async-start | bytes 524288 | tf_op jit(solution)/shard_map/psum | solution.py:85
  1028.9 619.8 %copy-start = (f32[256,256]{1,0:T(8,128)S(1)}, f32[256,256]{1,0:T(8,128)}, u32[]{:S(2)}) copy-start(f32[256,256]{1,0:T(8,128)} %get-tuple-element.766) | copy-start | bytes 786436
Sparse Core Ops, SparseCore 0:
  768.9 258.9 all-reduce.1
where the time goes:
time: 2090 us; the launch traced here: 2060 us
  local copies, waits for them, and re-layouts  1040 us (50%)
  other arithmetic  364 us (17%)
  waiting for transfers between devices  259 us (12%)
  loops' own time  209 us (10%)
  matrix products  171 us (8%)
    dynamic_slice x512, local copies, waits for them, and re-layouts, row_step(): pivot = lax.dynamic_slice_in_dim(r_row, row, 1, 0)[0]  478 us
    div x512, other arithmetic, row_step(): (unit - jnp.dot(beyond, inverse, precision=exact_mode, preferred_element_...  355 us
    psum x1, waiting for transfers between devices, factor_rows(): gram_one = lax.psum(gram_one, ('gx', 'gy'))  259 us
    another operation x1, loops' own time, cholesky_lower(): return lax.fori_loop(0, size_n, column_step, jnp.zeros_like(gram_mat))  189 us
    dynamic_slice x512, local copies, waits for them, and re-layouts, row_step(): r_row = lax.dynamic_slice_in_dim(r_upper, row, 1, 0)[0]  181 us
    dynamic_slice x256, local copies, waits for them, and re-layouts, column_step(): pivot = jnp.sqrt(lax.dynamic_slice_in_dim(vector, col, 1, 0)[0])  166 us
    dynamic_update_slice x256, local copies, waits for them, and re-layouts, column_step(): return lax.dynamic_update_slice_in_dim(lower, column[:, None], col, 1)  157 us
    dot_general x512, matrix products, row_step(): jnp.dot(beyond, inverse, precision=exact_mode, preferred_element_type=jnp...  93.6 us

commit v1 on v0

v1 whole, which is shorter than its diff:
```python
import functools
import math

import jax
import jax.numpy as jnp
from jax import lax
from jax.experimental import pallas as pl
from jax.experimental.pallas import tpu as pltpu
from jax.sharding import Mesh, PartitionSpec as P

F32 = jnp.float32
exact = lax.Precision.HIGHEST
N = 256
SUB = 8
PANEL = 64


def mm(a, b, dims=((1,), (0,))):
    return lax.dot_general(a, b, (dims, ((), ())), precision=exact, preferred_element_type=F32)


def iota(shape, dim):
    return lax.broadcasted_iota(jnp.int32, shape, dim)


def lane_group_copy(x, k):
    half = x.shape[1] // 128
    out = []
    for h in range(half):
        part = x[:, 128 * h : 128 * (h + 1)]
        idx = (iota(part.shape, 1) // SUB) * SUB + k
        out.append(jnp.take_along_axis(part, idx, axis=1))
    return jnp.concatenate(out, axis=1)


def upper_inverse(p_ref):
    lane = iota((SUB, N), 1)
    sub = iota((SUB, N), 0)
    diag = jnp.zeros((SUB, N), F32)
    for b in range(N // SUB):
        diag = jnp.where(lane // SUB == b, p_ref[SUB * b : SUB * (b + 1), :], diag)
    rest = jnp.where(lane % SUB == sub, 1.0, 0.0)
    small = jnp.zeros((SUB, N), F32)
    for k in reversed(range(SUB)):
        column = lane_group_copy(diag, k)
        row = jnp.broadcast_to(rest[k : k + 1, :] / column[k : k + 1, :], (SUB, N))
        small = jnp.where(sub == k, row, small)
        if k:
            rest = rest - jnp.where(sub < k, column, 0.0) * row
    row_all, col_all = iota((N, N), 0), iota((N, N), 1)
    inverse = jnp.where(row_all // SUB == col_all // SUB, jnp.concatenate([small] * (N // SUB), axis=0), 0.0)
    upper = p_ref[...]
    size = SUB
    while size < N:
        pair = (row_all // (2 * size) == col_all // (2 * size)) & (row_all // size < col_all // size)
        inverse = inverse - mm(inverse, mm(jnp.where(pair, upper, 0.0), inverse))
        size *= 2
    return inverse


def first_kernel(counts_ref, span_ref, prior_ref, y_ref, gram_ref, inverse_ref):
    live = counts_ref[0]
    inverse_ref[...] = upper_inverse(prior_ref)
    block = 512
    gram_ref[...] = jnp.zeros((N, N), F32)
    for b in range(span_ref.shape[0] // block):
        start = b * block

        @pl.when(start < live)
        def _():
            rows = span_ref[start : start + block, :]
            keep = iota((block, N), 0) + start < live
            image = mm(jnp.where(keep, rows, 0.0), inverse_ref[...])
            y_ref[start : start + block, :] = image
            gram_ref[...] += mm(image, image, ((0,), (0,)))

        @pl.when(start >= live)
        def _():
            y_ref[start : start + block, :] = jnp.zeros((block, N), F32)


def eliminate_panel(m_ref, r_ref, p):
    base = p * PANEL
    groups = PANEL // SUB
    lane = iota((SUB, N), 1)
    sub = iota((SUB, N), 0)
    sub1 = iota((SUB, 128), 0)
    for t in range(groups):
        top = base + t * SUB
        cols = []
        for k in range(SUB):
            cols.append([
                jnp.broadcast_to(m_ref[base + g * SUB : base + (g + 1) * SUB, top + k : top + k + 1], (SUB, 128))
                for g in range(t, groups)
            ])
        s = {}
        for k in range(SUB):
            for i in range(k, SUB):
                s[i, k] = jnp.broadcast_to(cols[k][0][i : i + 1, :], (SUB, 128))
        scale = []
        low = {}
        for k in range(SUB):
            r = lax.rsqrt(s[k, k])
            scale.append(r)
            for i in range(k + 1, SUB):
                low[i, k] = s[i, k] * r
            for j in range(k + 1, SUB):
                for i in range(j, SUB):
                    s[i, j] = s[i, j] - low[i, k] * low[j, k]
            for g in range(1, groups - t):
                cols[k][g] = cols[k][g] * r
                for j in range(k + 1, SUB):
                    cols[j][g] = cols[j][g] - cols[k][g] * low[j, k]
        half = top // 128
        own = slice(128 * half, 128 * (half + 1))
        lane_own = iota((SUB, 128), 1) + 128 * half
        rows = []
        twin = []
        for k in range(SUB):
            full = jnp.broadcast_to(m_ref[top + k : top + k + 1, :], (SUB, N))
            part = jnp.where(
                (lane_own >= top) & (lane_own < top + SUB),
                jnp.where(lane_own == top + k, 1.0, 0.0),
                full[:, own],
            )
            for j in range(k):
                c = low[k, j]
                full = full - jnp.concatenate([c, c], axis=1) * rows[j]
                part = part - c * twin[j]
            r = scale[k]
            rows.append(full * jnp.concatenate([r, r], axis=1))
            twin.append(part * r)
        w_true = rows[0]
        w_own = twin[0]
        for k in range(1, SUB):
            w_true = jnp.where(sub == k, rows[k], w_true)
            w_own = jnp.where(sub1 == k, twin[k], w_own)
        r_ref[top : top + SUB, :] = jnp.where(lane >= top + sub, w_true, 0.0)
        w_parts = [w_true[:, :128], w_true[:, 128:]]
        w_parts[half] = w_own
        m_ref[top : top + SUB, :] = jnp.concatenate(w_parts, axis=1)
        for g in range(1, groups - t):
            at = slice(base + (t + g) * SUB, base + (t + g + 1) * SUB)
            for h in range(2):
                old = m_ref[at, 128 * h : 128 * (h + 1)]
                if h == half:
                    old = jnp.where((lane_own >= top) & (lane_own < top + SUB), 0.0, old)
                total = None
                for k in range(SUB):
                    row = twin[k] if h == half else rows[k][:, 128 * h : 128 * (h + 1)]
                    term = cols[k][g] * row
                    total = term if total is None else total + term
                m_ref[at, 128 * h : 128 * (h + 1)] = old - total


def factor(m_ref, r_ref):
    for p in range(N // PANEL):
        eliminate_panel(m_ref, r_ref, p)
        base, below = p * PANEL, (p + 1) * PANEL
        if below < N:
            w = m_ref[base:below, :]
            lane = iota((PANEL, N), 1)
            ahead = (lane < below) & (lane > base + iota((PANEL, N), 0))
            gain = mm(w[:, below:] if below % 128 == 0 else w, jnp.where(ahead, 0.0, w), ((0,), (0,)))
            if below % 128:
                gain = gain[below:, :]
            lane = iota((N - below, N), 1)
            old = jnp.where((lane >= base) & (lane < below), 0.0, m_ref[below:, :])
            m_ref[below:, :] = old - gain


def second_kernel(row_scale, packed_ref, prior_ref, y_ref, r_out, q_out, m_ref, r_ref):
    m_ref[0:64, :] = packed_ref[0:64, :]
    second = packed_ref[64:128, :]
    m_ref[64:128, :] = second
    m_ref[128:160, 128:256] = packed_ref[128:160, 128:256]
    m_ref[160:192, 128:256] = packed_ref[128:160, 0:128]
    m_ref[192:256, 128:256] = pltpu.roll(second[:, 0:128], 64, 1)
    m_ref[128:256, 0:128] = jnp.zeros((128, 128), F32)
    row_all, col_all = iota((N, N), 0), iota((N, N), 1)
    m_ref[...] = jnp.where(
        row_all // PANEL <= col_all // PANEL,
        m_ref[...] + jnp.where(row_all == col_all, 1.0, 0.0),
        0.0,
    )
    factor(m_ref, r_ref)
    r_out[...] = mm(r_ref[...], prior_ref[...]) * (1.0 / row_scale)
    low_inverse = jnp.where(row_all >= col_all, m_ref[...], 0.0) * row_scale
    r_ref[...] = low_inverse
    block = 512
    for b in range(y_ref.shape[0] // block):
        at = slice(b * block, (b + 1) * block)
        q_out[at, :] = mm(y_ref[at, :], r_ref[...], ((1,), (1,)))


def swap(value, axis, pairs):
    return lax.ppermute(value, axis, [p for a, b in pairs for p in ((a, b), (b, a))])


RING4 = (((0, 1), (2, 3)), ((1, 2), (3, 0)))
RING8 = (((0, 1), (2, 3), (4, 5), (6, 7)), ((1, 2), (3, 4), (5, 6), (7, 0)), ((0, 3), (1, 6), (2, 5), (4, 7)))


def sum_all(packed):
    one = lax.axis_index("core") == 1
    half = packed.shape[0] // 2
    first, last = packed[:half], packed[half:]
    mine = jnp.where(one, last, first) + swap(jnp.where(one, first, last), "core", ((0, 1),))
    for axis, turns in (("x", RING4), ("y", RING4), ("z", RING8)):
        for pairs in turns:
            mine = mine + swap(mine, axis, pairs)
    other = swap(mine, "core", ((0, 1),))
    return jnp.concatenate([jnp.where(one, other, mine), jnp.where(one, mine, other)], axis=0)


def pack(gram):
    lane = iota((64, N), 1)
    second = jnp.where(lane < 64, jnp.roll(gram[192:256, :], 64, axis=1), gram[64:128, :])
    third = jnp.concatenate([gram[160:192, 128:256], gram[128:160, 128:256]], axis=1)
    return jnp.concatenate([gram[0:64, :], second, third], axis=0)


VMEM = pl.BlockSpec(memory_space=pltpu.VMEM)
SMEM = pl.BlockSpec(memory_space=pltpu.SMEM)
PARAMS = pltpu.CompilerParams(vmem_limit_bytes=40 * 2**20)


def stage_one(span, prior, counts):
    rows = span.shape[0]
    return pl.pallas_call(
        first_kernel,
        out_shape=(jax.ShapeDtypeStruct((rows, N), F32), jax.ShapeDtypeStruct((N, N), F32)),
        in_specs=[SMEM, VMEM, VMEM],
        out_specs=(VMEM, VMEM),
        scratch_shapes=[pltpu.VMEM((N, N), F32)],
        compiler_params=PARAMS,
    )(counts, span, prior)


def stage_two(packed, prior, y, row_scale):
    rows = y.shape[0]
    return pl.pallas_call(
        functools.partial(second_kernel, row_scale),
        out_shape=(jax.ShapeDtypeStruct((N, N), F32), jax.ShapeDtypeStruct((rows, N), F32)),
        in_specs=[VMEM, VMEM, VMEM],
        out_specs=(VMEM, VMEM),
        scratch_shapes=[pltpu.VMEM((N, N), F32), pltpu.VMEM((N, N), F32)],
        compiler_params=PARAMS,
    )(packed, prior, y)


def per_device(span, prior, counts, row_scale):
    y, gram = stage_one(span, prior, counts)
    return stage_two(sum_all(pack(gram)), prior, y, row_scale)


def solution(mesh):
    fine = Mesh(mesh.devices.reshape(4, 2, 4, 8), ("x", "core", "y", "z"))
    split = ("x", "core", "y", "z")

    def run(span, prior, counts):
        row_scale = math.sqrt(span.shape[0])
        return jax.shard_map(
            functools.partial(per_device, row_scale=row_scale),
            mesh=fine,
            in_specs=(P(split, None), P(), P(split)),
            out_specs=(P(), P(split, None)),
            check_vma=False,
        )(span, prior, counts)

    return run
```

time: 2090 us -> 74 us (0.04); the launches traced: 2060 us -> 73.5 us
  local copies, waits for them, and re-layouts: 1040 us -> 2.62 us
  other arithmetic: 364 us -> 0.23 us
  waiting for transfers between devices: 259 us -> 17.6 us
  loops' own time: 209 us -> 0 us
  matrix products: 171 us -> 0 us
  starting transfers between devices: 0.04 us -> 31.9 us
    dynamic_slice x1536 -> x0, local copies, waits for them, and re-layouts: 827 us -> none  [the longest x512 478 us: row_step(): pivot = lax.dynamic_slice_in_dim(r_row, row, 1, 0)[0]]
    div x512 -> x0, other arithmetic: 355 us -> none  [row_step(): (unit - jnp.dot(beyond, inverse, precision=exact_mode, preferred_element_...]
    psum x1 -> x0, waiting for transfers between devices: 259 us -> none  [factor_rows(): gram_one = lax.psum(gram_one, ('gx', 'gy'))]
    another operation x5 -> x0, loops' own time: 209 us -> none  [the longest x1 189 us: cholesky_lower(): return lax.fori_loop(0, size_n, column_step, jnp.zeros_like(gram_mat))]
    dynamic_update_slice x768 -> x0, local copies, waits for them, and re-layouts: 179 us -> none  [the longest x256 157 us: column_step(): return lax.dynamic_update_slice_in_dim(lower, column[:, None], col, 1)]
    dot_general x775 -> x0, matrix products: 171 us -> none  [the longest x512 93.6 us: row_step(): jnp.dot(beyond, inverse, precision=exact_mode, preferred_element_type=jnp...]
    broadcast_in_dim x256 -> x0, local copies, waits for them, and re-layouts: 34.2 us -> none  [column_step(): return lax.dynamic_update_slice_in_dim(lower, column[:, None], col, 1)]
    ppermute x0 -> x9, starting transfers between devices: none -> 31.9 us  [swap(): lax.ppermute(value, axis, [p for a, b in pairs for p in ((a, b), (b, a))])]
where the time goes in v1:
time: 74 us; the launch traced here: 73.5 us
  starting transfers between devices  31.9 us (43%)
  Pallas kernels  19.8 us (27%)
  waiting for transfers between devices  17.6 us (24%)
  local copies, waits for them, and re-layouts  2.62 us (4%)
  between operations  1.39 us (2%)
    ppermute x9, starting transfers between devices, swap(): lax.ppermute(value, axis, [p for a, b in pairs for p in ((a, b), (b, a))])  31.9 us
    ppermute x9, waiting for transfers between devices, swap(): lax.ppermute(value, axis, [p for a, b in pairs for p in ((a, b), (b, a))])  17.6 us
    pallas_call x1, Pallas kernels, stage_two(): pl.pallas_call(functools.partial(second_kernel, row_scale), out_shape=(ja...  12.3 us
    pallas_call x1, Pallas kernels, stage_one(): pl.pallas_call(first_kernel, out_shape=(jax.ShapeDtypeStruct((rows, N), F...  7.5 us
    unnamed x6, local copies, waits for them, and re-layouts  2.54 us
  transfers between devices with their start and end apart: 9, of which 9 were waited for; matrix products, arithmetic and copies ran while one was open for 0% of the time, Pallas kernels for 0%

profile of v1, /device:TPU:1, one launch (start us, length us, event | category | flops | bytes accessed | tf_op | source)
XLA Modules:
  0.0 73.5 jit_solution(7870812823684466591)
XLA Ops:
  1.3 0.0 copy-start
  1.3 1.6 %copy-done = f32[2048,256]{1,0:T(8,128)S(1)} copy-done((f32[2048,256]{1,0:T(8,128)S(1)}, f32[2048,256]{1,0:T(8,128)}, u32[]{:S(2)}) %copy-start) | copy-done | bytes 2097176
  2.9 0.0 copy-start.1
  2.9 0.9 %copy-done.1 = f32[256,256]{1,0:T(8,128)S(1)} copy-done((f32[256,256]{1,0:T(8,128)S(1)}, f32[256,256]{1,0:T(8,128)}, u32[]{:S(2)}) %copy-start.1) | copy-done | bytes 262168
  3.8 7.5 %shard_map.50 = (f32[2048,256]{1,0:T(8,128)S(1)}, f32[256,256]{1,0:T(8,128)S(1)}) custom-call(s32[1]{0:T(128)S(6)} %copy.5.counts_ref, f32[2048,256]{1,0:T(8,128)S(1)} %copy-done, f32[256,256]{1,0:T(8,128)S(1)} %copy-done.1), custom_call_target="tpu_custom_call" | custom-call | tf_op jit(solution)/shard_map/pallas_call | solution.py:230
  11.3 0.0 copy-start.2
  11.4 0.1 slice.31
  11.5 0.1 fusion.1
  11.6 3.3 %collective-permute-start = (f32[80,256]{1,0:T(8,128)S(1)}, f32[80,256]{1,0:T(8,128)S(1)}, u32[]{:S(2)}, u32[]{:S(2)}) collective-permute-start(f32[80,256]{1,0:T(8,128)S(1)} %fusion), channel_id=1, source_target_pairs={{0,32},{32,0},{1,33},{33,1},{2,34},{34,2},{3,35},{35,3},{4,36},{36... | collective-permute-start | bytes 245768 | tf_op jit(solution)/shard_map/ppermute | solution.py:197
  14.9 0.9 %collective-permute-done = f32[80,256]{1,0:T(8,128)S(1)} collective-permute-done((f32[80,256]{1,0:T(8,128)S(1)}, f32[80,256]{1,0:T(8,128)S(1)}, u32[]{:S(2)}, u32[]{:S(2)}) %collective-permute-start) | collective-permute-done | bytes 81952 | tf_op jit(solution)/shard_map/ppermute | solution.py:197
  15.8 1.1 %collective-permute-start.1 = (f32[80,256]{1,0:T(8,128)S(1)}, f32[80,256]{1,0:T(8,128)S(1)}, u32[]{:S(2)}, u32[]{:S(2)}) collective-permute-start(f32[80,256]{1,0:T(8,128)S(1)} %select_add_fusion), channel_id=1, source_target_pairs={{0,64},{64,0},{128,192},{192,128},{1,65},{65,1},{129,193},{193,129... | collective-permute-start | bytes 245768 | tf_op jit(solution)/shard_map/ppermute | solution.py:197
  16.9 2.7 %collective-permute-done.1 = f32[80,256]{1,0:T(8,128)S(1)} collective-permute-done((f32[80,256]{1,0:T(8,128)S(1)}, f32[80,256]{1,0:T(8,128)S(1)}, u32[]{:S(2)}, u32[]{:S(2)}) %collective-permute-start.1) | collective-permute-done | bytes 81952 | tf_op jit(solution)/shard_map/ppermute | solution.py:197
  19.6 4.4 %collective-permute-start.2 = (f32[80,256]{1,0:T(8,128)S(1)}, f32[80,256]{1,0:T(8,128)S(1)}, u32[]{:S(2)}, u32[]{:S(2)}) collective-permute-start(f32[80,256]{1,0:T(8,128)S(1)} %add.25), channel_id=1, source_target_pairs={{64,128},{128,64},{192,0},{0,192},{65,129},{129,65},{193,1},{1,193... | collective-permute-start | bytes 245768 | tf_op jit(solution)/shard_map/ppermute | solution.py:197
  24.0 1.8 %collective-permute-done.2 = f32[80,256]{1,0:T(8,128)S(1)} collective-permute-done((f32[80,256]{1,0:T(8,128)S(1)}, f32[80,256]{1,0:T(8,128)S(1)}, u32[]{:S(2)}, u32[]{:S(2)}) %collective-permute-start.2) | collective-permute-done | bytes 81952 | tf_op jit(solution)/shard_map/ppermute | solution.py:197
  25.9 1.9 %collective-permute-start.3 = (f32[80,256]{1,0:T(8,128)S(1)}, f32[80,256]{1,0:T(8,128)S(1)}, u32[]{:S(2)}, u32[]{:S(2)}) collective-permute-start(f32[80,256]{1,0:T(8,128)S(1)} %add.26), channel_id=1, source_target_pairs={{0,8},{8,0},{16,24},{24,16},{1,9},{9,1},{17,25},{25,17},{2,10},{10... | collective-permute-start | bytes 245768 | tf_op jit(solution)/shard_map/ppermute | solution.py:197
  27.7 1.8 %collective-permute-done.3 = f32[80,256]{1,0:T(8,128)S(1)} collective-permute-done((f32[80,256]{1,0:T(8,128)S(1)}, f32[80,256]{1,0:T(8,128)S(1)}, u32[]{:S(2)}, u32[]{:S(2)}) %collective-permute-start.3) | collective-permute-done | bytes 81952 | tf_op jit(solution)/shard_map/ppermute | solution.py:197
  29.6 2.8 %collective-permute-start.4 = (f32[80,256]{1,0:T(8,128)S(1)}, f32[80,256]{1,0:T(8,128)S(1)}, u32[]{:S(2)}, u32[]{:S(2)}) collective-permute-start(f32[80,256]{1,0:T(8,128)S(1)} %add.27), channel_id=1, source_target_pairs={{8,16},{16,8},{24,0},{0,24},{9,17},{17,9},{25,1},{1,25},{10,18},{1... | collective-permute-start | bytes 245768 | tf_op jit(solution)/shard_map/ppermute | solution.py:197
  32.4 1.8 %collective-permute-done.4 = f32[80,256]{1,0:T(8,128)S(1)} collective-permute-done((f32[80,256]{1,0:T(8,128)S(1)}, f32[80,256]{1,0:T(8,128)S(1)}, u32[]{:S(2)}, u32[]{:S(2)}) %collective-permute-start.4) | collective-permute-done | bytes 81952 | tf_op jit(solution)/shard_map/ppermute | solution.py:197
  34.2 3.6 %collective-permute-start.5 = (f32[80,256]{1,0:T(8,128)S(1)}, f32[80,256]{1,0:T(8,128)S(1)}, u32[]{:S(2)}, u32[]{:S(2)}) collective-permute-start(f32[80,256]{1,0:T(8,128)S(1)} %add.28), channel_id=1, source_target_pairs={{0,1},{1,0},{2,3},{3,2},{4,5},{5,4},{6,7},{7,6},{8,9},{9,8},{10,11... | collective-permute-start | bytes 245768 | tf_op jit(solution)/shard_map/ppermute | solution.py:197
  37.9 1.8 %collective-permute-done.5 = f32[80,256]{1,0:T(8,128)S(1)} collective-permute-done((f32[80,256]{1,0:T(8,128)S(1)}, f32[80,256]{1,0:T(8,128)S(1)}, u32[]{:S(2)}, u32[]{:S(2)}) %collective-permute-start.5) | collective-permute-done | bytes 81952 | tf_op jit(solution)/shard_map/ppermute | solution.py:197
  39.7 5.6 %collective-permute-start.6 = (f32[80,256]{1,0:T(8,128)S(1)}, f32[80,256]{1,0:T(8,128)S(1)}, u32[]{:S(2)}, u32[]{:S(2)}) collective-permute-start(f32[80,256]{1,0:T(8,128)S(1)} %add.29), channel_id=1, source_target_pairs={{1,2},{2,1},{3,4},{4,3},{5,6},{6,5},{7,0},{0,7},{9,10},{10,9},{11,... | collective-permute-start | bytes 245768 | tf_op jit(solution)/shard_map/ppermute | solution.py:197
  45.3 1.8 %collective-permute-done.6 = f32[80,256]{1,0:T(8,128)S(1)} collective-permute-done((f32[80,256]{1,0:T(8,128)S(1)}, f32[80,256]{1,0:T(8,128)S(1)}, u32[]{:S(2)}, u32[]{:S(2)}) %collective-permute-start.6) | collective-permute-done | bytes 81952 | tf_op jit(solution)/shard_map/ppermute | solution.py:197
  47.2 2.1 %collective-permute-start.7 = (f32[80,256]{1,0:T(8,128)S(1)}, f32[80,256]{1,0:T(8,128)S(1)}, u32[]{:S(2)}, u32[]{:S(2)}) collective-permute-start(f32[80,256]{1,0:T(8,128)S(1)} %add.30), channel_id=1, source_target_pairs={{0,3},{3,0},{1,6},{6,1},{2,5},{5,2},{4,7},{7,4},{8,11},{11,8},{9,1... | collective-permute-start | bytes 245768 | tf_op jit(solution)/shard_map/ppermute | solution.py:197
  49.2 4.0 %collective-permute-done.7 = f32[80,256]{1,0:T(8,128)S(1)} collective-permute-done((f32[80,256]{1,0:T(8,128)S(1)}, f32[80,256]{1,0:T(8,128)S(1)}, u32[]{:S(2)}, u32[]{:S(2)}) %collective-permute-start.7) | collective-permute-done | bytes 81952 | tf_op jit(solution)/shard_map/ppermute | solution.py:197
  53.2 7.0 %collective-permute-start.8 = (f32[80,256]{1,0:T(8,128)S(1)}, f32[80,256]{1,0:T(8,128)S(1)}, u32[]{:S(2)}, u32[]{:S(2)}) collective-permute-start(f32[80,256]{1,0:T(8,128)S(1)} %add.31), channel_id=1, source_target_pairs={{0,32},{32,0},{1,33},{33,1},{2,34},{34,2},{3,35},{35,3},{4,36},{36... | collective-permute-start | bytes 245768 | tf_op jit(solution)/shard_map/ppermute | solution.py:197
  60.3 0.9 %collective-permute-done.8 = f32[80,256]{1,0:T(8,128)S(1)} collective-permute-done((f32[80,256]{1,0:T(8,128)S(1)}, f32[80,256]{1,0:T(8,128)S(1)}, u32[]{:S(2)}, u32[]{:S(2)}) %collective-permute-start.8) | collective-permute-done | bytes 81952 | tf_op jit(solution)/shard_map/ppermute | solution.py:197
  61.2 0.0 copy-done.2
  61.2 12.3 %shard_map.51 = (f32[256,256]{1,0:T(8,128)}, f32[2048,256]{1,0:T(8,128)}) custom-call(f32[160,256]{1,0:T(8,128)S(1)} %pad_maximum_fusion.packed_ref, f32[256,256]{1,0:T(8,128)S(1)} %copy-done.2, f32[2048,256]{1,0:T(8,128)S(1)} %get-tuple-element.5.y_ref), custom_call_target="tpu_custom_call" | custom-call | tf_op jit(solution)/shard_map/pallas_call | solution.py:242
  (14 shorter events, 0.2 us)
Async XLA Ops:
  1.3 1.6 %copy-start = (f32[2048,256]{1,0:T(8,128)S(1)}, f32[2048,256]{1,0:T(8,128)}, u32[]{:S(2)}) copy-start(f32[2048,256]{1,0:T(8,128)} %span_ref.1) | copy-start | bytes 6291460
  2.9 0.9 %copy-start.1 = (f32[256,256]{1,0:T(8,128)S(1)}, f32[256,256]{1,0:T(8,128)}, u32[]{:S(2)}) copy-start(f32[256,256]{1,0:T(8,128)} %prior_ref.3) | copy-start | bytes 786436
  11.3 49.9 %copy-start.2 = (f32[256,256]{1,0:T(8,128)S(1)}, f32[256,256]{1,0:T(8,128)}, u32[]{:S(2)}) copy-start(f32[256,256]{1,0:T(8,128)} %prior_ref.3) | copy-start | bytes 786436
  11.6 4.3 %collective-permute-start = (f32[80,256]{1,0:T(8,128)S(1)}, f32[80,256]{1,0:T(8,128)S(1)}, u32[]{:S(2)}, u32[]{:S(2)}) collective-permute-start(f32[80,256]{1,0:T(8,128)S(1)} %fusion), channel_id=1, source_target_pairs={{0,32},{32,0},{1,33},{33,1},{2,34},{34,2},{3,35},{35,3},{4,36},{36... | collective-permute-start | bytes 245768 | tf_op jit(solution)/shard_map/ppermute | solution.py:197
  15.8 3.8 %collective-permute-start.1 = (f32[80,256]{1,0:T(8,128)S(1)}, f32[80,256]{1,0:T(8,128)S(1)}, u32[]{:S(2)}, u32[]{:S(2)}) collective-permute-start(f32[80,256]{1,0:T(8,128)S(1)} %select_add_fusion), channel_id=1, source_target_pairs={{0,64},{64,0},{128,192},{192,128},{1,65},{65,1},{129,193},{193,129... | collective-permute-start | bytes 245768 | tf_op jit(solution)/shard_map/ppermute | solution.py:197
  19.6 6.3 %collective-permute-start.2 = (f32[80,256]{1,0:T(8,128)S(1)}, f32[80,256]{1,0:T(8,128)S(1)}, u32[]{:S(2)}, u32[]{:S(2)}) collective-permute-start(f32[80,256]{1,0:T(8,128)S(1)} %add.25), channel_id=1, source_target_pairs={{64,128},{128,64},{192,0},{0,192},{65,129},{129,65},{193,1},{1,193... | collective-permute-start | bytes 245768 | tf_op jit(solution)/shard_map/ppermute | solution.py:197
  25.9 3.7 %collective-permute-start.3 = (f32[80,256]{1,0:T(8,128)S(1)}, f32[80,256]{1,0:T(8,128)S(1)}, u32[]{:S(2)}, u32[]{:S(2)}) collective-permute-start(f32[80,256]{1,0:T(8,128)S(1)} %add.26), channel_id=1, source_target_pairs={{0,8},{8,0},{16,24},{24,16},{1,9},{9,1},{17,25},{25,17},{2,10},{10... | collective-permute-start | bytes 245768 | tf_op jit(solution)/shard_map/ppermute | solution.py:197
  29.6 4.6 %collective-permute-start.4 = (f32[80,256]{1,0:T(8,128)S(1)}, f32[80,256]{1,0:T(8,128)S(1)}, u32[]{:S(2)}, u32[]{:S(2)}) collective-permute-start(f32[80,256]{1,0:T(8,128)S(1)} %add.27), channel_id=1, source_target_pairs={{8,16},{16,8},{24,0},{0,24},{9,17},{17,9},{25,1},{1,25},{10,18},{1... | collective-permute-start | bytes 245768 | tf_op jit(solution)/shard_map/ppermute | solution.py:197
  34.2 5.5 %collective-permute-start.5 = (f32[80,256]{1,0:T(8,128)S(1)}, f32[80,256]{1,0:T(8,128)S(1)}, u32[]{:S(2)}, u32[]{:S(2)}) collective-permute-start(f32[80,256]{1,0:T(8,128)S(1)} %add.28), channel_id=1, source_target_pairs={{0,1},{1,0},{2,3},{3,2},{4,5},{5,4},{6,7},{7,6},{8,9},{9,8},{10,11... | collective-permute-start | bytes 245768 | tf_op jit(solution)/shard_map/ppermute | solution.py:197
  39.7 7.4 %collective-permute-start.6 = (f32[80,256]{1,0:T(8,128)S(1)}, f32[80,256]{1,0:T(8,128)S(1)}, u32[]{:S(2)}, u32[]{:S(2)}) collective-permute-start(f32[80,256]{1,0:T(8,128)S(1)} %add.29), channel_id=1, source_target_pairs={{1,2},{2,1},{3,4},{4,3},{5,6},{6,5},{7,0},{0,7},{9,10},{10,9},{11,... | collective-permute-start | bytes 245768 | tf_op jit(solution)/shard_map/ppermute | solution.py:197
  47.2 6.1 %collective-permute-start.7 = (f32[80,256]{1,0:T(8,128)S(1)}, f32[80,256]{1,0:T(8,128)S(1)}, u32[]{:S(2)}, u32[]{:S(2)}) collective-permute-start(f32[80,256]{1,0:T(8,128)S(1)} %add.30), channel_id=1, source_target_pairs={{0,3},{3,0},{1,6},{6,1},{2,5},{5,2},{4,7},{7,4},{8,11},{11,8},{9,1... | collective-permute-start | bytes 245768 | tf_op jit(solution)/shard_map/ppermute | solution.py:197
  53.2 8.0 %collective-permute-start.8 = (f32[80,256]{1,0:T(8,128)S(1)}, f32[80,256]{1,0:T(8,128)S(1)}, u32[]{:S(2)}, u32[]{:S(2)}) collective-permute-start(f32[80,256]{1,0:T(8,128)S(1)} %add.31), channel_id=1, source_target_pairs={{0,32},{32,0},{1,33},{33,1},{2,34},{34,2},{3,35},{35,3},{4,36},{36... | collective-permute-start | bytes 245768 | tf_op jit(solution)/shard_map/ppermute | solution.py:197

commit v2 on v1

--- a/solution.py
+++ b/solution.py
@@ -9,6 +9,8 @@
 from jax.sharding import Mesh, PartitionSpec as P
 
 F32 = jnp.float32
+BF16 = jnp.bfloat16
+BLOCK = 512
 exact = lax.Precision.HIGHEST
 N = 256
 SUB = 8
@@ -17,6 +19,24 @@
 
 def mm(a, b, dims=((1,), (0,))):
     return lax.dot_general(a, b, (dims, ((), ())), precision=exact, preferred_element_type=F32)
+
+
+def cut(x, parts):
+    out = []
+    for _ in range(parts):
+        out.append(x.astype(BF16))
+        x = x - out[-1].astype(F32)
+    return out
+
+
+def dot(a, b, dims=((1,), (0,))):
+    return lax.dot_general(a, b, (dims, ((), ())), preferred_element_type=F32)
+
+
+def mm6(left, right):
+    a1, a2, a3 = left
+    b1, b2, b3 = right
+    return dot(jnp.concatenate([a3, a2, a1, a2, a1, a1], axis=1), jnp.concatenate([b1, b2, b3, b1, b2, b1], axis=0))
 
 
 def iota(shape, dim):
@@ -33,7 +53,7 @@
     return jnp.concatenate(out, axis=1)
 
 
-def upper_inverse(p_ref):
+def small_inverses(p_ref):
     lane = iota((SUB, N), 1)
     sub = iota((SUB, N), 0)
     diag = jnp.zeros((SUB, N), F32)
@@ -47,36 +67,69 @@
         small = jnp.where(sub == k, row, small)
         if k:
             rest = rest - jnp.where(sub < k, column, 0.0) * row
-    row_all, col_all = iota((N, N), 0), iota((N, N), 1)
-    inverse = jnp.where(row_all // SUB == col_all // SUB, jnp.concatenate([small] * (N // SUB), axis=0), 0.0)
-    upper = p_ref[...]
-    size = SUB
-    while size < N:
-        pair = (row_all // (2 * size) == col_all // (2 * size)) & (row_all // size < col_all // size)
-        inverse = inverse - mm(inverse, mm(jnp.where(pair, upper, 0.0), inverse))
-        size *= 2
-    return inverse
-
-
-def first_kernel(counts_ref, span_ref, prior_ref, y_ref, gram_ref, inverse_ref):
+    return small
+
+
+def upper_inverse(p_ref, small):
+    half = N // 2
+    row, col = iota((half, half), 0), iota((half, half), 1)
+    corners = []
+    for h in range(2):
+        part = slice(half * h, half * (h + 1))
+        inverse = jnp.where(row // SUB == col // SUB, jnp.concatenate([small[:, part]] * (half // SUB), axis=0), 0.0)
+        upper = p_ref[part, part]
+        size = SUB
+        while size < half:
+            pair = (row // (2 * size) == col // (2 * size)) & (row // size < col // size)
+            known = cut(inverse, 3)
+            inverse = inverse - mm6(known, cut(mm6(cut(jnp.where(pair, upper, 0.0), 3), known), 3))
+            size *= 2
+        corners.append(inverse)
+    known = [cut(c, 3) for c in corners]
+    cross = mm6(known[0], cut(mm6(cut(p_ref[:half, half:], 3), known[1]), 3))
+    top = jnp.concatenate([corners[0], -cross], axis=1)
+    return jnp.concatenate([top, jnp.concatenate([jnp.zeros((half, half), F32), corners[1]], axis=1)], axis=0)
+
+
+def first_kernel(
+    counts_ref, span_ref, prior_ref, high_out, low_out, packed_ref, rows_ref, parts_ref, high_ref, low_ref, in_sems, out_sems
+):
     live = counts_ref[0]
-    inverse_ref[...] = upper_inverse(prior_ref)
-    block = 512
-    gram_ref[...] = jnp.zeros((N, N), F32)
-    for b in range(span_ref.shape[0] // block):
-        start = b * block
-
-        @pl.when(start < live)
-        def _():
-            rows = span_ref[start : start + block, :]
-            keep = iota((block, N), 0) + start < live
-            image = mm(jnp.where(keep, rows, 0.0), inverse_ref[...])
-            y_ref[start : start + block, :] = image
-            gram_ref[...] += mm(image, image, ((0,), (0,)))
-
-        @pl.when(start >= live)
-        def _():
-            y_ref[start : start + block, :] = jnp.zeros((block, N), F32)
+    count = span_ref.shape[0] // BLOCK
+    blocks = [pl.ds(b * BLOCK, BLOCK) for b in range(count)]
+    copies = [pltpu.make_async_copy(span_ref.at[at, :], rows_ref.at[at, :], in_sems.at[b]) for b, at in enumerate(blocks)]
+    for copy in copies:
+        copy.start()
+    small = small_inverses(prior_ref)
+    for copy in copies:
+        copy.wait()
+    for b, at in enumerate(blocks):
+        keep = iota((BLOCK, N), 0) + b * BLOCK < live
+        for i, part in enumerate(cut(jnp.where(keep, rows_ref[at, :], 0.0), 3)):
+            parts_ref[at, i * N : (i + 1) * N] = part
+    b1, b2, b3 = cut(upper_inverse(prior_ref, small), 3)
+    right = jnp.concatenate([b1, b2, b3, b1, b2, b1], axis=0)
+    writes = []
+    sums = None
+    for b, at in enumerate(blocks):
+        a1, a2, a3 = (parts_ref[at, i * N : (i + 1) * N] for i in range(3))
+        high, low = cut(dot(jnp.concatenate([a3, a2, a1, a2, a1, a1], axis=1), right), 2)
+        high_ref[at, :] = high
+        low_ref[at, :] = low
+        for i, (source, target) in enumerate(((high_ref, high_out), (low_ref, low_out))):
+            writes.append(pltpu.make_async_copy(source.at[at, :], target.at[at, :], out_sems.at[2 * b + i]))
+            writes[-1].start()
+        gain = dot(high.T, jnp.concatenate([high, low], axis=1))
+        sums = gain if sums is None else sums + gain
+    mixed = sums[:, N:]
+    gram = sums[:, :N] + (mixed + mixed.T)
+    packed_ref[0:64, :] = gram[0:64, :]
+    packed_ref[64:128, :] = gram[64:128, :]
+    packed_ref[64:128, 0:64] = pltpu.roll(gram[192:256, 128:256], 64, 1)[:, 0:64]
+    packed_ref[128:160, 0:128] = gram[160:192, 128:256]
+    packed_ref[128:160, 128:256] = gram[128:160, 128:256]
+    for write in writes:
+        write.wait()
 
 
 def eliminate_panel(m_ref, r_ref, p):
@@ -169,7 +222,7 @@
             m_ref[below:, :] = old - gain
 
 
-def second_kernel(row_scale, packed_ref, prior_ref, y_ref, r_out, q_out, m_ref, r_ref):
+def second_kernel(row_scale, packed_ref, prior_ref, high_ref, low_ref, r_out, q_out, m_ref, r_ref, q_ref, sems):
     m_ref[0:64, :] = packed_ref[0:64, :]
     second = packed_ref[64:128, :]
     m_ref[64:128, :] = second
@@ -184,13 +237,22 @@
         0.0,
     )
     factor(m_ref, r_ref)
+    b1, b2 = cut(jnp.where(row_all >= col_all, m_ref[...], 0.0).T * row_scale, 2)
+    right = jnp.concatenate([b1, b2, b1], axis=0)
+    copies = []
+    for b in range(high_ref.shape[0] // BLOCK):
+        at = slice(b * BLOCK, (b + 1) * BLOCK)
+        high = high_ref[at, :]
+        q_ref[at, :] = dot(jnp.concatenate([low_ref[at, :], high, high], axis=1), right)
+        copies.append(
+            pltpu.make_async_copy(
+                q_ref.at[pl.ds(b * BLOCK, BLOCK), :], q_out.at[pl.ds(b * BLOCK, BLOCK), :], sems.at[b]
+            )
+        )
+        copies[-1].start()
     r_out[...] = mm(r_ref[...], prior_ref[...]) * (1.0 / row_scale)
-    low_inverse = jnp.where(row_all >= col_all, m_ref[...], 0.0) * row_scale
-    r_ref[...] = low_inverse
-    block = 512
-    for b in range(y_ref.shape[0] // block):
-        at = slice(b * block, (b + 1) * block)
-        q_out[at, :] = mm(y_ref[at, :], r_ref[...], ((1,), (1,)))
+    for copy in copies:
+        copy.wait()
 
 
 def swap(value, axis, pairs):
@@ -213,45 +275,56 @@
     return jnp.concatenate([jnp.where(one, other, mine), jnp.where(one, mine, other)], axis=0)
 
 
-def pack(gram):
-    lane = iota((64, N), 1)
-    second = jnp.where(lane < 64, jnp.roll(gram[192:256, :], 64, axis=1), gram[64:128, :])
-    third = jnp.concatenate([gram[160:192, 128:256], gram[128:160, 128:256]], axis=1)
-    return jnp.concatenate([gram[0:64, :], second, third], axis=0)
-
-
 VMEM = pl.BlockSpec(memory_space=pltpu.VMEM)
+HBM = pl.BlockSpec(memory_space=pltpu.HBM)
 SMEM = pl.BlockSpec(memory_space=pltpu.SMEM)
 PARAMS = pltpu.CompilerParams(vmem_limit_bytes=40 * 2**20)
+FIRST = pltpu.CompilerParams(vmem_limit_bytes=60 * 2**20)
 
 
 def stage_one(span, prior, counts):
     rows = span.shape[0]
     return pl.pallas_call(
         first_kernel,
-        out_shape=(jax.ShapeDtypeStruct((rows, N), F32), jax.ShapeDtypeStruct((N, N), F32)),
-        in_specs=[SMEM, VMEM, VMEM],
-        out_specs=(VMEM, VMEM),
-        scratch_shapes=[pltpu.VMEM((N, N), F32)],
-        compiler_params=PARAMS,
+        out_shape=(
+            jax.ShapeDtypeStruct((rows, N), BF16),
+            jax.ShapeDtypeStruct((rows, N), BF16),
+            jax.ShapeDtypeStruct((160, N), F32),
+        ),
+        in_specs=[SMEM, HBM, VMEM],
+        out_specs=(HBM, HBM, VMEM),
+        scratch_shapes=[
+            pltpu.VMEM((rows, N), F32),
+            pltpu.VMEM((rows, 3 * N), BF16),
+            pltpu.VMEM((rows, N), BF16),
+            pltpu.VMEM((rows, N), BF16),
+            pltpu.SemaphoreType.DMA((rows // BLOCK,)),
+            pltpu.SemaphoreType.DMA((2 * rows // BLOCK,)),
+        ],
+        compiler_params=FIRST,
     )(counts, span, prior)
 
 
-def stage_two(packed, prior, y, row_scale):
-    rows = y.shape[0]
+def stage_two(packed, prior, high, low, row_scale):
+    rows = high.shape[0]
     return pl.pallas_call(
         functools.partial(second_kernel, row_scale),
         out_shape=(jax.ShapeDtypeStruct((N, N), F32), jax.ShapeDtypeStruct((rows, N), F32)),
-        in_specs=[VMEM, VMEM, VMEM],
-        out_specs=(VMEM, VMEM),
-        scratch_shapes=[pltpu.VMEM((N, N), F32), pltpu.VMEM((N, N), F32)],
+        in_specs=[VMEM, VMEM, VMEM, VMEM],
+        out_specs=(VMEM, HBM),
+        scratch_shapes=[
+            pltpu.VMEM((N, N), F32),
+            pltpu.VMEM((N, N), F32),
+            pltpu.VMEM((rows, N), F32),
+            pltpu.SemaphoreType.DMA((rows // BLOCK,)),
+        ],
         compiler_params=PARAMS,
-    )(packed, prior, y)
+    )(packed, prior, high, low)
 
 
 def per_device(span, prior, counts, row_scale):
-    y, gram = stage_one(span, prior, counts)
-    return stage_two(sum_all(pack(gram)), prior, y, row_scale)
+    high, low, packed = stage_one(span, prior, counts)
+    return stage_two(sum_all(packed), prior, high, low, row_scale)
 
 
 def solution(mesh):

time: 74 us -> 70.4 us (0.951)
  starting transfers between devices: 31.9 us -> 18.1 us
  waiting for transfers between devices: 17.6 us -> 25.8 us
  Pallas kernels: 19.8 us -> 22.6 us
  local copies, waits for them, and re-layouts: 2.62 us -> 0.01 us
  other arithmetic: 0.23 us -> 2.13 us
    ppermute x9, starting transfers between devices: 31.9 us -> 18.1 us  [swap(): lax.ppermute(value, axis, [p for a, b in pairs for p in ((a, b), (b, a))])]
    ppermute x9, waiting for transfers between devices: 17.6 us -> 25.8 us  [swap(): lax.ppermute(value, axis, [p for a, b in pairs for p in ((a, b), (b, a))])]
    pallas_call x1, Pallas kernels: 7.5 us -> 11 us  [stage_one(): pl.pallas_call(first_kernel, out_shape=(jax.ShapeDtypeStruct((rows, N), B...]
    unnamed x6, local copies, waits for them, and re-layouts: 2.54 us -> 0.01 us
    select_n x1, other arithmetic: 0.01 us -> 1.09 us  [sum_all(): jnp.where(one, first, last)]
    add x1, other arithmetic: 0.02 us -> 0.94 us  [sum_all(): jnp.where(one, last, first)]
where the time goes in v2:
time: 70.4 us; the launch traced here: 70.2 us
  waiting for transfers between devices  25.8 us (37%)
  Pallas kernels  22.6 us (32%)
  starting transfers between devices  18.1 us (26%)
  other arithmetic  2.13 us (3%)
  between operations  1.57 us (2%)
    ppermute x9, waiting for transfers between devices, swap(): lax.ppermute(value, axis, [p for a, b in pairs for p in ((a, b), (b, a))])  25.8 us
    ppermute x9, starting transfers between devices, swap(): lax.ppermute(value, axis, [p for a, b in pairs for p in ((a, b), (b, a))])  18.1 us
    pallas_call x1, Pallas kernels, stage_two(): pl.pallas_call(functools.partial(second_kernel, row_scale), out_shape=(ja...  11.6 us
    pallas_call x1, Pallas kernels, stage_one(): pl.pallas_call(first_kernel, out_shape=(jax.ShapeDtypeStruct((rows, N), B...  11 us
  transfers between devices with their start and end apart: 9, of which 9 were waited for; matrix products, arithmetic and copies ran while one was open for 0% of the time, Pallas kernels for 0%

profile of v2, /device:TPU:1, one launch (start us, length us, event | category | flops | bytes accessed | tf_op | source)
XLA Modules:
  0.0 70.2 jit_solution(5841503671030514273)
XLA Ops:
  1.3 0.0 copy-start
  1.3 11.0 %shard_map.50 = (bf16[2048,256]{1,0:T(8,128)(2,1)}, bf16[2048,256]{1,0:T(8,128)(2,1)}, f32[160,256]{1,0:T(8,128)}) custom-call(s32[1]{0:T(128)S(6)} %copy.5.counts_ref, f32[2048,256]{1,0:T(8,128)} %span_ref.1, f32[256,256]{1,0:T(8,128)} %prior_ref.3), custom_call_target="tpu_custom_call" | custom-call | tf_op jit(solution)/shard_map/pallas_call | solution.py:287
  12.3 0.0 copy-start.1
  12.3 0.0 copy-start.2
  12.4 1.1 %slice_select_fusion = f32[80,256]{1,0:T(8,128)S(1)} fusion(f32[160,256]{1,0:T(8,128)} %get-tuple-element.5, pred[]{:T(512)S(6)} %eq.3), kind=kLoop, calls=%fused_computation.2 | loop fusion | flops 20480 | bytes 245761 | tf_op jit(solution)/shard_map/jit(_where)/select_n | solution.py:270
  13.4 3.3 %collective-permute-start = (f32[80,256]{1,0:T(8,128)S(1)}, f32[80,256]{1,0:T(8,128)S(1)}, u32[]{:S(2)}, u32[]{:S(2)}) collective-permute-start(f32[80,256]{1,0:T(8,128)S(1)} %slice_select_fusion), channel_id=1, source_target_pairs={{0,32},{32,0},{1,33},{33,1},{2,34},{34,2},{3,35},{35,3},{4,36},{36... | collective-permute-start | bytes 245768 | tf_op jit(solution)/shard_map/ppermute | solution.py:259
  16.8 0.9 %collective-permute-done = f32[80,256]{1,0:T(8,128)S(1)} collective-permute-done((f32[80,256]{1,0:T(8,128)S(1)}, f32[80,256]{1,0:T(8,128)S(1)}, u32[]{:S(2)}, u32[]{:S(2)}) %collective-permute-start) | collective-permute-done | bytes 81952 | tf_op jit(solution)/shard_map/ppermute | solution.py:259
  17.7 0.9 %select_add_fusion = f32[80,256]{1,0:T(8,128)S(1)} fusion(f32[80,256]{1,0:T(8,128)S(1)} %collective-permute-done, f32[160,256]{1,0:T(8,128)} %get-tuple-element.5, pred[]{:T(512)S(6)} %eq.3), kind=kLoop, calls=%fused_computation.1 | loop fusion | flops 40960 | bytes 327681 | tf_op jit(solution)/shard_map/add | solution.py:270
  18.6 0.1 collective-permute-start.1
  18.7 3.7 %collective-permute-done.1 = f32[80,256]{1,0:T(8,128)S(1)} collective-permute-done((f32[80,256]{1,0:T(8,128)S(1)}, f32[80,256]{1,0:T(8,128)S(1)}, u32[]{:S(2)}, u32[]{:S(2)}) %collective-permute-start.1) | collective-permute-done | bytes 81952 | tf_op jit(solution)/shard_map/ppermute | solution.py:259
  22.4 0.8 %collective-permute-start.2 = (f32[80,256]{1,0:T(8,128)S(1)}, f32[80,256]{1,0:T(8,128)S(1)}, u32[]{:S(2)}, u32[]{:S(2)}) collective-permute-start(f32[80,256]{1,0:T(8,128)S(1)} %add.25), channel_id=1, source_target_pairs={{64,128},{128,64},{192,0},{0,192},{65,129},{129,65},{193,1},{1,193... | collective-permute-start | bytes 245768 | tf_op jit(solution)/shard_map/ppermute | solution.py:259
  23.2 3.8 %collective-permute-done.2 = f32[80,256]{1,0:T(8,128)S(1)} collective-permute-done((f32[80,256]{1,0:T(8,128)S(1)}, f32[80,256]{1,0:T(8,128)S(1)}, u32[]{:S(2)}, u32[]{:S(2)}) %collective-permute-start.2) | collective-permute-done | bytes 81952 | tf_op jit(solution)/shard_map/ppermute | solution.py:259
  27.0 0.1 collective-permute-start.3
  27.1 3.3 %collective-permute-done.3 = f32[80,256]{1,0:T(8,128)S(1)} collective-permute-done((f32[80,256]{1,0:T(8,128)S(1)}, f32[80,256]{1,0:T(8,128)S(1)}, u32[]{:S(2)}, u32[]{:S(2)}) %collective-permute-start.3) | collective-permute-done | bytes 81952 | tf_op jit(solution)/shard_map/ppermute | solution.py:259
  30.4 1.1 %collective-permute-start.4 = (f32[80,256]{1,0:T(8,128)S(1)}, f32[80,256]{1,0:T(8,128)S(1)}, u32[]{:S(2)}, u32[]{:S(2)}) collective-permute-start(f32[80,256]{1,0:T(8,128)S(1)} %add.27), channel_id=1, source_target_pairs={{8,16},{16,8},{24,0},{0,24},{9,17},{17,9},{25,1},{1,25},{10,18},{1... | collective-permute-start | bytes 245768 | tf_op jit(solution)/shard_map/ppermute | solution.py:259
  31.5 3.5 %collective-permute-done.4 = f32[80,256]{1,0:T(8,128)S(1)} collective-permute-done((f32[80,256]{1,0:T(8,128)S(1)}, f32[80,256]{1,0:T(8,128)S(1)}, u32[]{:S(2)}, u32[]{:S(2)}) %collective-permute-start.4) | collective-permute-done | bytes 81952 | tf_op jit(solution)/shard_map/ppermute | solution.py:259
  35.0 0.1 collective-permute-start.5
  35.1 3.6 %collective-permute-done.5 = f32[80,256]{1,0:T(8,128)S(1)} collective-permute-done((f32[80,256]{1,0:T(8,128)S(1)}, f32[80,256]{1,0:T(8,128)S(1)}, u32[]{:S(2)}, u32[]{:S(2)}) %collective-permute-start.5) | collective-permute-done | bytes 81952 | tf_op jit(solution)/shard_map/ppermute | solution.py:259
  38.7 4.0 %collective-permute-start.6 = (f32[80,256]{1,0:T(8,128)S(1)}, f32[80,256]{1,0:T(8,128)S(1)}, u32[]{:S(2)}, u32[]{:S(2)}) collective-permute-start(f32[80,256]{1,0:T(8,128)S(1)} %add.29), channel_id=1, source_target_pairs={{1,2},{2,1},{3,4},{4,3},{5,6},{6,5},{7,0},{0,7},{9,10},{10,9},{11,... | collective-permute-start | bytes 245768 | tf_op jit(solution)/shard_map/ppermute | solution.py:259
  42.7 1.8 %collective-permute-done.6 = f32[80,256]{1,0:T(8,128)S(1)} collective-permute-done((f32[80,256]{1,0:T(8,128)S(1)}, f32[80,256]{1,0:T(8,128)S(1)}, u32[]{:S(2)}, u32[]{:S(2)}) %collective-permute-start.6) | collective-permute-done | bytes 81952 | tf_op jit(solution)/shard_map/ppermute | solution.py:259
  44.5 1.7 %collective-permute-start.7 = (f32[80,256]{1,0:T(8,128)S(1)}, f32[80,256]{1,0:T(8,128)S(1)}, u32[]{:S(2)}, u32[]{:S(2)}) collective-permute-start(f32[80,256]{1,0:T(8,128)S(1)} %add.30), channel_id=1, source_target_pairs={{0,3},{3,0},{1,6},{6,1},{2,5},{5,2},{4,7},{7,4},{8,11},{11,8},{9,1... | collective-permute-start | bytes 245768 | tf_op jit(solution)/shard_map/ppermute | solution.py:259
  46.3 4.3 %collective-permute-done.7 = f32[80,256]{1,0:T(8,128)S(1)} collective-permute-done((f32[80,256]{1,0:T(8,128)S(1)}, f32[80,256]{1,0:T(8,128)S(1)}, u32[]{:S(2)}, u32[]{:S(2)}) %collective-permute-start.7) | collective-permute-done | bytes 81952 | tf_op jit(solution)/shard_map/ppermute | solution.py:259
  50.6 6.8 %collective-permute-start.8 = (f32[80,256]{1,0:T(8,128)S(1)}, f32[80,256]{1,0:T(8,128)S(1)}, u32[]{:S(2)}, u32[]{:S(2)}) collective-permute-start(f32[80,256]{1,0:T(8,128)S(1)} %add.31), channel_id=1, source_target_pairs={{0,32},{32,0},{1,33},{33,1},{2,34},{34,2},{3,35},{35,3},{4,36},{36... | collective-permute-start | bytes 245768 | tf_op jit(solution)/shard_map/ppermute | solution.py:259
  57.4 0.9 %collective-permute-done.8 = f32[80,256]{1,0:T(8,128)S(1)} collective-permute-done((f32[80,256]{1,0:T(8,128)S(1)}, f32[80,256]{1,0:T(8,128)S(1)}, u32[]{:S(2)}, u32[]{:S(2)}) %collective-permute-start.8) | collective-permute-done | bytes 81952 | tf_op jit(solution)/shard_map/ppermute | solution.py:259
  58.4 0.0 copy-done
  58.4 0.0 copy-done.1
  58.4 0.0 copy-done.2
  58.4 11.6 %shard_map.51 = (f32[256,256]{1,0:T(8,128)}, f32[2048,256]{1,0:T(8,128)}) custom-call(f32[160,256]{1,0:T(8,128)S(1)} %pad_maximum_fusion.packed_ref, f32[256,256]{1,0:T(8,128)S(1)} %copy-done, bf16[2048,256]{1,0:T(8,128)(2,1)S(1)} %copy-done.1, bf16[2048,256]{1,0:T(8,128)(2,1)S(1)} %copy-done.2), custom_call_target="tpu_custom_call" | custom-call | tf_op jit(solution)/shard_map/pallas_call | solution.py:310
  (9 shorter events, 0.1 us)
Async XLA Ops:
  1.3 57.1 %copy-start = (f32[256,256]{1,0:T(8,128)S(1)}, f32[256,256]{1,0:T(8,128)}, u32[]{:S(2)}) copy-start(f32[256,256]{1,0:T(8,128)} %prior_ref.3) | copy-start | bytes 786436
  12.3 46.1 %copy-start.1 = (bf16[2048,256]{1,0:T(8,128)(2,1)S(1)}, bf16[2048,256]{1,0:T(8,128)(2,1)}, u32[]{:S(2)}) copy-start(bf16[2048,256]{1,0:T(8,128)(2,1)} %get-tuple-element.6.high_ref) | copy-start | bytes 3145732
  12.3 46.1 %copy-start.2 = (bf16[2048,256]{1,0:T(8,128)(2,1)S(1)}, bf16[2048,256]{1,0:T(8,128)(2,1)}, u32[]{:S(2)}) copy-start(bf16[2048,256]{1,0:T(8,128)(2,1)} %get-tuple-element.7.low_ref) | copy-start | bytes 3145732
  13.4 4.3 %collective-permute-start = (f32[80,256]{1,0:T(8,128)S(1)}, f32[80,256]{1,0:T(8,128)S(1)}, u32[]{:S(2)}, u32[]{:S(2)}) collective-permute-start(f32[80,256]{1,0:T(8,128)S(1)} %slice_select_fusion), channel_id=1, source_target_pairs={{0,32},{32,0},{1,33},{33,1},{2,34},{34,2},{3,35},{35,3},{4,36},{36... | collective-permute-start | bytes 245768 | tf_op jit(solution)/shard_map/ppermute | solution.py:259
  18.6 3.8 %collective-permute-start.1 = (f32[80,256]{1,0:T(8,128)S(1)}, f32[80,256]{1,0:T(8,128)S(1)}, u32[]{:S(2)}, u32[]{:S(2)}) collective-permute-start(f32[80,256]{1,0:T(8,128)S(1)} %select_add_fusion), channel_id=1, source_target_pairs={{0,64},{64,0},{128,192},{192,128},{1,65},{65,1},{129,193},{193,129... | collective-permute-start | bytes 245768 | tf_op jit(solution)/shard_map/ppermute | solution.py:259
  22.4 4.6 %collective-permute-start.2 = (f32[80,256]{1,0:T(8,128)S(1)}, f32[80,256]{1,0:T(8,128)S(1)}, u32[]{:S(2)}, u32[]{:S(2)}) collective-permute-start(f32[80,256]{1,0:T(8,128)S(1)} %add.25), channel_id=1, source_target_pairs={{64,128},{128,64},{192,0},{0,192},{65,129},{129,65},{193,1},{1,193... | collective-permute-start | bytes 245768 | tf_op jit(solution)/shard_map/ppermute | solution.py:259
  27.0 3.4 %collective-permute-start.3 = (f32[80,256]{1,0:T(8,128)S(1)}, f32[80,256]{1,0:T(8,128)S(1)}, u32[]{:S(2)}, u32[]{:S(2)}) collective-permute-start(f32[80,256]{1,0:T(8,128)S(1)} %add.26), channel_id=1, source_target_pairs={{0,8},{8,0},{16,24},{24,16},{1,9},{9,1},{17,25},{25,17},{2,10},{10... | collective-permute-start | bytes 245768 | tf_op jit(solution)/shard_map/ppermute | solution.py:259
  30.4 4.6 %collective-permute-start.4 = (f32[80,256]{1,0:T(8,128)S(1)}, f32[80,256]{1,0:T(8,128)S(1)}, u32[]{:S(2)}, u32[]{:S(2)}) collective-permute-start(f32[80,256]{1,0:T(8,128)S(1)} %add.27), channel_id=1, source_target_pairs={{8,16},{16,8},{24,0},{0,24},{9,17},{17,9},{25,1},{1,25},{10,18},{1... | collective-permute-start | bytes 245768 | tf_op jit(solution)/shard_map/ppermute | solution.py:259
  35.0 3.7 %collective-permute-start.5 = (f32[80,256]{1,0:T(8,128)S(1)}, f32[80,256]{1,0:T(8,128)S(1)}, u32[]{:S(2)}, u32[]{:S(2)}) collective-permute-start(f32[80,256]{1,0:T(8,128)S(1)} %add.28), channel_id=1, source_target_pairs={{0,1},{1,0},{2,3},{3,2},{4,5},{5,4},{6,7},{7,6},{8,9},{9,8},{10,11... | collective-permute-start | bytes 245768 | tf_op jit(solution)/shard_map/ppermute | solution.py:259
  38.7 5.8 %collective-permute-start.6 = (f32[80,256]{1,0:T(8,128)S(1)}, f32[80,256]{1,0:T(8,128)S(1)}, u32[]{:S(2)}, u32[]{:S(2)}) collective-permute-start(f32[80,256]{1,0:T(8,128)S(1)} %add.29), channel_id=1, source_target_pairs={{1,2},{2,1},{3,4},{4,3},{5,6},{6,5},{7,0},{0,7},{9,10},{10,9},{11,... | collective-permute-start | bytes 245768 | tf_op jit(solution)/shard_map/ppermute | solution.py:259
  44.5 6.0 %collective-permute-start.7 = (f32[80,256]{1,0:T(8,128)S(1)}, f32[80,256]{1,0:T(8,128)S(1)}, u32[]{:S(2)}, u32[]{:S(2)}) collective-permute-start(f32[80,256]{1,0:T(8,128)S(1)} %add.30), channel_id=1, source_target_pairs={{0,3},{3,0},{1,6},{6,1},{2,5},{5,2},{4,7},{7,4},{8,11},{11,8},{9,1... | collective-permute-start | bytes 245768 | tf_op jit(solution)/shard_map/ppermute | solution.py:259
  50.6 7.8 %collective-permute-start.8 = (f32[80,256]{1,0:T(8,128)S(1)}, f32[80,256]{1,0:T(8,128)S(1)}, u32[]{:S(2)}, u32[]{:S(2)}) collective-permute-start(f32[80,256]{1,0:T(8,128)S(1)} %add.31), channel_id=1, source_target_pairs={{0,32},{32,0},{1,33},{33,1},{2,34},{34,2},{3,35},{35,3},{4,36},{36... | collective-permute-start | bytes 245768 | tf_op jit(solution)/shard_map/ppermute | solution.py:259

commit v3 on v2

--- a/solution.py
+++ b/solution.py
@@ -132,38 +132,42 @@
         write.wait()
 
 
+def spread(ref, row, col):
+    return jnp.broadcast_to(ref[row : row + SUB, col : col + 1], (SUB, 128))
+
+
 def eliminate_panel(m_ref, r_ref, p):
     base = p * PANEL
     groups = PANEL // SUB
     lane = iota((SUB, N), 1)
     sub = iota((SUB, N), 0)
     sub1 = iota((SUB, 128), 0)
+    ahead = None
     for t in range(groups):
         top = base + t * SUB
-        cols = []
-        for k in range(SUB):
-            cols.append([
-                jnp.broadcast_to(m_ref[base + g * SUB : base + (g + 1) * SUB, top + k : top + k + 1], (SUB, 128))
+        cols = [
+            [
+                ahead[k] if g == t and ahead else spread(m_ref, base + g * SUB, top + k)
                 for g in range(t, groups)
-            ])
-        s = {}
-        for k in range(SUB):
-            for i in range(k, SUB):
-                s[i, k] = jnp.broadcast_to(cols[k][0][i : i + 1, :], (SUB, 128))
+            ]
+            for k in range(SUB)
+        ]
         scale = []
         low = {}
         for k in range(SUB):
-            r = lax.rsqrt(s[k, k])
+            r = lax.rsqrt(jnp.broadcast_to(cols[k][0][k : k + 1, :], (SUB, 128)))
             scale.append(r)
-            for i in range(k + 1, SUB):
-                low[i, k] = s[i, k] * r
+            cols[k] = [c * r for c in cols[k]]
             for j in range(k + 1, SUB):
-                for i in range(j, SUB):
-                    s[i, j] = s[i, j] - low[i, k] * low[j, k]
-            for g in range(1, groups - t):
-                cols[k][g] = cols[k][g] * r
-                for j in range(k + 1, SUB):
-                    cols[j][g] = cols[j][g] - cols[k][g] * low[j, k]
+                low[j, k] = jnp.broadcast_to(cols[k][0][j : j + 1, :], (SUB, 128))
+                cols[j] = [c - d * low[j, k] for c, d in zip(cols[j], cols[k])]
+        if t + 1 < groups:
+            ahead = []
+            for j in range(SUB):
+                block = spread(m_ref, top + SUB, top + SUB + j)
+                for k in range(SUB):
+                    block = block - cols[k][1] * jnp.broadcast_to(cols[k][1][j : j + 1, :], (SUB, 128))
+                ahead.append(block)
         half = top // 128
         own = slice(128 * half, 128 * (half + 1))
         lane_own = iota((SUB, 128), 1) + 128 * half
@@ -214,9 +218,15 @@
             w = m_ref[base:below, :]
             lane = iota((PANEL, N), 1)
             ahead = (lane < below) & (lane > base + iota((PANEL, N), 0))
-            gain = mm(w[:, below:] if below % 128 == 0 else w, jnp.where(ahead, 0.0, w), ((0,), (0,)))
+            a1, a2, a3 = cut(w[:, 128:] if below >= 128 else w, 3)
+            b1, b2, b3 = cut(jnp.where(ahead, 0.0, w), 3)
+            gain = dot(
+                jnp.concatenate([a3, a2, a1, a2, a1, a1], axis=0),
+                jnp.concatenate([b1, b2, b3, b1, b2, b1], axis=0),
+                ((0,), (0,)),
+            )
             if below % 128:
-                gain = gain[below:, :]
+                gain = gain[64:, :]
             lane = iota((N - below, N), 1)
             old = jnp.where((lane >= base) & (lane < below), 0.0, m_ref[below:, :])
             m_ref[below:, :] = old - gain
@@ -279,7 +289,7 @@
 HBM = pl.BlockSpec(memory_space=pltpu.HBM)
 SMEM = pl.BlockSpec(memory_space=pltpu.SMEM)
 PARAMS = pltpu.CompilerParams(vmem_limit_bytes=40 * 2**20)
-FIRST = pltpu.CompilerParams(vmem_limit_bytes=60 * 2**20)
+FIRST = pltpu.CompilerParams(vmem_limit_bytes=50 * 2**20)
 
 
 def stage_one(span, prior, counts):

time: 70.4 us -> 64.9 us (0.922)
  Pallas kernels: 22.6 us -> 18.3 us
  other arithmetic: 2.13 us -> 0.13 us
  local copies, waits for them, and re-layouts: 0.01 us -> 0.94 us
    pallas_call x1, Pallas kernels: 11.6 us -> 7.78 us  [stage_two(): pl.pallas_call(functools.partial(second_kernel, row_scale), out_shape=(ja...]
    select_n x1, other arithmetic: 1.09 us -> 0.01 us  [sum_all(): jnp.where(one, first, last)]
    unnamed x6 -> x2, local copies, waits for them, and re-layouts: 0.01 us -> 0.94 us
    add x1, other arithmetic: 0.94 us -> 0.02 us  [sum_all(): jnp.where(one, last, first)]
where the time goes in v3:
time: 64.9 us; the launch traced here: 64.7 us
  waiting for transfers between devices  25.8 us (40%)
  Pallas kernels  18.3 us (28%)
  starting transfers between devices  18.1 us (28%)
  between operations  1.53 us (2%)
  local copies, waits for them, and re-layouts  0.94 us (1%)
    ppermute x9, waiting for transfers between devices, swap(): lax.ppermute(value, axis, [p for a, b in pairs for p in ((a, b), (b, a))])  25.8 us
    ppermute x9, starting transfers between devices, swap(): lax.ppermute(value, axis, [p for a, b in pairs for p in ((a, b), (b, a))])  18.1 us
    pallas_call x1, Pallas kernels, stage_one(): pl.pallas_call(first_kernel, out_shape=(jax.ShapeDtypeStruct((rows, N), B...  10.5 us
    pallas_call x1, Pallas kernels, stage_two(): pl.pallas_call(functools.partial(second_kernel, row_scale), out_shape=(ja...  7.78 us
  transfers between devices with their start and end apart: 9, of which 9 were waited for; matrix products, arithmetic and copies ran while one was open for 0% of the time, Pallas kernels for 0%

profile of v3, /device:TPU:1, one launch (start us, length us, event | category | flops | bytes accessed | tf_op | source)
XLA Modules:
  0.0 64.7 jit_solution(9716893478506469569)
XLA Ops:
  1.3 0.0 copy-start
  1.3 0.9 %copy-done = f32[256,256]{1,0:T(8,128)S(1)} copy-done((f32[256,256]{1,0:T(8,128)S(1)}, f32[256,256]{1,0:T(8,128)}, u32[]{:S(2)}) %copy-start) | copy-done | bytes 262168
  2.2 10.5 %shard_map.50 = (bf16[2048,256]{1,0:T(8,128)(2,1)S(1)}, bf16[2048,256]{1,0:T(8,128)(2,1)S(1)}, f32[160,256]{1,0:T(8,128)S(1)}) custom-call(s32[1]{0:T(128)S(6)} %copy.5.counts_ref, f32[2048,256]{1,0:T(8,128)} %span_ref.1, f32[256,256]{1,0:T(8,128)S(1)} %copy-done), custom_call_target="tpu_custom_call" | custom-call | tf_op jit(solution)/shard_map/pallas_call | solution.py:297
  12.7 3.3 %collective-permute-start = (f32[80,256]{1,0:T(8,128)S(1)}, f32[80,256]{1,0:T(8,128)S(1)}, u32[]{:S(2)}, u32[]{:S(2)}) collective-permute-start(f32[80,256]{1,0:T(8,128)S(1)} %slice_select_fusion), channel_id=1, source_target_pairs={{0,32},{32,0},{1,33},{33,1},{2,34},{34,2},{3,35},{35,3},{4,36},{36... | collective-permute-start | bytes 245768 | tf_op jit(solution)/shard_map/ppermute | solution.py:269
  16.1 0.9 %collective-permute-done = f32[80,256]{1,0:T(8,128)S(1)} collective-permute-done((f32[80,256]{1,0:T(8,128)S(1)}, f32[80,256]{1,0:T(8,128)S(1)}, u32[]{:S(2)}, u32[]{:S(2)}) %collective-permute-start) | collective-permute-done | bytes 81952 | tf_op jit(solution)/shard_map/ppermute | solution.py:269
  17.0 0.1 collective-permute-start.1
  17.1 3.7 %collective-permute-done.1 = f32[80,256]{1,0:T(8,128)S(1)} collective-permute-done((f32[80,256]{1,0:T(8,128)S(1)}, f32[80,256]{1,0:T(8,128)S(1)}, u32[]{:S(2)}, u32[]{:S(2)}) %collective-permute-start.1) | collective-permute-done | bytes 81952 | tf_op jit(solution)/shard_map/ppermute | solution.py:269
  20.8 0.8 %collective-permute-start.2 = (f32[80,256]{1,0:T(8,128)S(1)}, f32[80,256]{1,0:T(8,128)S(1)}, u32[]{:S(2)}, u32[]{:S(2)}) collective-permute-start(f32[80,256]{1,0:T(8,128)S(1)} %add.25), channel_id=1, source_target_pairs={{64,128},{128,64},{192,0},{0,192},{65,129},{129,65},{193,1},{1,193... | collective-permute-start | bytes 245768 | tf_op jit(solution)/shard_map/ppermute | solution.py:269
  21.6 3.8 %collective-permute-done.2 = f32[80,256]{1,0:T(8,128)S(1)} collective-permute-done((f32[80,256]{1,0:T(8,128)S(1)}, f32[80,256]{1,0:T(8,128)S(1)}, u32[]{:S(2)}, u32[]{:S(2)}) %collective-permute-start.2) | collective-permute-done | bytes 81952 | tf_op jit(solution)/shard_map/ppermute | solution.py:269
  25.4 0.1 collective-permute-start.3
  25.5 3.3 %collective-permute-done.3 = f32[80,256]{1,0:T(8,128)S(1)} collective-permute-done((f32[80,256]{1,0:T(8,128)S(1)}, f32[80,256]{1,0:T(8,128)S(1)}, u32[]{:S(2)}, u32[]{:S(2)}) %collective-permute-start.3) | collective-permute-done | bytes 81952 | tf_op jit(solution)/shard_map/ppermute | solution.py:269
  28.8 1.1 %collective-permute-start.4 = (f32[80,256]{1,0:T(8,128)S(1)}, f32[80,256]{1,0:T(8,128)S(1)}, u32[]{:S(2)}, u32[]{:S(2)}) collective-permute-start(f32[80,256]{1,0:T(8,128)S(1)} %add.27), channel_id=1, source_target_pairs={{8,16},{16,8},{24,0},{0,24},{9,17},{17,9},{25,1},{1,25},{10,18},{1... | collective-permute-start | bytes 245768 | tf_op jit(solution)/shard_map/ppermute | solution.py:269
  29.9 3.5 %collective-permute-done.4 = f32[80,256]{1,0:T(8,128)S(1)} collective-permute-done((f32[80,256]{1,0:T(8,128)S(1)}, f32[80,256]{1,0:T(8,128)S(1)}, u32[]{:S(2)}, u32[]{:S(2)}) %collective-permute-start.4) | collective-permute-done | bytes 81952 | tf_op jit(solution)/shard_map/ppermute | solution.py:269
  33.4 0.1 collective-permute-start.5
  33.5 3.6 %collective-permute-done.5 = f32[80,256]{1,0:T(8,128)S(1)} collective-permute-done((f32[80,256]{1,0:T(8,128)S(1)}, f32[80,256]{1,0:T(8,128)S(1)}, u32[]{:S(2)}, u32[]{:S(2)}) %collective-permute-start.5) | collective-permute-done | bytes 81952 | tf_op jit(solution)/shard_map/ppermute | solution.py:269
  37.1 4.0 %collective-permute-start.6 = (f32[80,256]{1,0:T(8,128)S(1)}, f32[80,256]{1,0:T(8,128)S(1)}, u32[]{:S(2)}, u32[]{:S(2)}) collective-permute-start(f32[80,256]{1,0:T(8,128)S(1)} %add.29), channel_id=1, source_target_pairs={{1,2},{2,1},{3,4},{4,3},{5,6},{6,5},{7,0},{0,7},{9,10},{10,9},{11,... | collective-permute-start | bytes 245768 | tf_op jit(solution)/shard_map/ppermute | solution.py:269
  41.1 1.8 %collective-permute-done.6 = f32[80,256]{1,0:T(8,128)S(1)} collective-permute-done((f32[80,256]{1,0:T(8,128)S(1)}, f32[80,256]{1,0:T(8,128)S(1)}, u32[]{:S(2)}, u32[]{:S(2)}) %collective-permute-start.6) | collective-permute-done | bytes 81952 | tf_op jit(solution)/shard_map/ppermute | solution.py:269
  42.9 1.7 %collective-permute-start.7 = (f32[80,256]{1,0:T(8,128)S(1)}, f32[80,256]{1,0:T(8,128)S(1)}, u32[]{:S(2)}, u32[]{:S(2)}) collective-permute-start(f32[80,256]{1,0:T(8,128)S(1)} %add.30), channel_id=1, source_target_pairs={{0,3},{3,0},{1,6},{6,1},{2,5},{5,2},{4,7},{7,4},{8,11},{11,8},{9,1... | collective-permute-start | bytes 245768 | tf_op jit(solution)/shard_map/ppermute | solution.py:269
  44.6 4.3 %collective-permute-done.7 = f32[80,256]{1,0:T(8,128)S(1)} collective-permute-done((f32[80,256]{1,0:T(8,128)S(1)}, f32[80,256]{1,0:T(8,128)S(1)}, u32[]{:S(2)}, u32[]{:S(2)}) %collective-permute-start.7) | collective-permute-done | bytes 81952 | tf_op jit(solution)/shard_map/ppermute | solution.py:269
  49.0 6.8 %collective-permute-start.8 = (f32[80,256]{1,0:T(8,128)S(1)}, f32[80,256]{1,0:T(8,128)S(1)}, u32[]{:S(2)}, u32[]{:S(2)}) collective-permute-start(f32[80,256]{1,0:T(8,128)S(1)} %add.31), channel_id=1, source_target_pairs={{0,32},{32,0},{1,33},{33,1},{2,34},{34,2},{3,35},{35,3},{4,36},{36... | collective-permute-start | bytes 245768 | tf_op jit(solution)/shard_map/ppermute | solution.py:269
  55.8 0.9 %collective-permute-done.8 = f32[80,256]{1,0:T(8,128)S(1)} collective-permute-done((f32[80,256]{1,0:T(8,128)S(1)}, f32[80,256]{1,0:T(8,128)S(1)}, u32[]{:S(2)}, u32[]{:S(2)}) %collective-permute-start.8) | collective-permute-done | bytes 81952 | tf_op jit(solution)/shard_map/ppermute | solution.py:269
  56.8 7.8 %shard_map.51 = (f32[256,256]{1,0:T(8,128)}, f32[2048,256]{1,0:T(8,128)}) custom-call(f32[160,256]{1,0:T(8,128)S(1)} %pad_maximum_fusion.packed_ref, f32[256,256]{1,0:T(8,128)S(1)} %copy-done, bf16[2048,256]{1,0:T(8,128)(2,1)S(1)} %get-tuple-element.6.high_ref, bf16[2048,256]{1,0:T(8,128)(2,1)S(1)} %get-tuple-element.7.low_ref), custom_call_target="tpu_custom_call" | custom-call | tf_op jit(solution)/shard_map/pallas_call | solution.py:320
  (11 shorter events, 0.1 us)
Async XLA Ops:
  1.3 1.0 %copy-start = (f32[256,256]{1,0:T(8,128)S(1)}, f32[256,256]{1,0:T(8,128)}, u32[]{:S(2)}) copy-start(f32[256,256]{1,0:T(8,128)} %prior_ref.3) | copy-start | bytes 786436
  12.7 4.3 %collective-permute-start = (f32[80,256]{1,0:T(8,128)S(1)}, f32[80,256]{1,0:T(8,128)S(1)}, u32[]{:S(2)}, u32[]{:S(2)}) collective-permute-start(f32[80,256]{1,0:T(8,128)S(1)} %slice_select_fusion), channel_id=1, source_target_pairs={{0,32},{32,0},{1,33},{33,1},{2,34},{34,2},{3,35},{35,3},{4,36},{36... | collective-permute-start | bytes 245768 | tf_op jit(solution)/shard_map/ppermute | solution.py:269
  17.0 3.8 %collective-permute-start.1 = (f32[80,256]{1,0:T(8,128)S(1)}, f32[80,256]{1,0:T(8,128)S(1)}, u32[]{:S(2)}, u32[]{:S(2)}) collective-permute-start(f32[80,256]{1,0:T(8,128)S(1)} %select_add_fusion), channel_id=1, source_target_pairs={{0,64},{64,0},{128,192},{192,128},{1,65},{65,1},{129,193},{193,129... | collective-permute-start | bytes 245768 | tf_op jit(solution)/shard_map/ppermute | solution.py:269
  20.8 4.6 %collective-permute-start.2 = (f32[80,256]{1,0:T(8,128)S(1)}, f32[80,256]{1,0:T(8,128)S(1)}, u32[]{:S(2)}, u32[]{:S(2)}) collective-permute-start(f32[80,256]{1,0:T(8,128)S(1)} %add.25), channel_id=1, source_target_pairs={{64,128},{128,64},{192,0},{0,192},{65,129},{129,65},{193,1},{1,193... | collective-permute-start | bytes 245768 | tf_op jit(solution)/shard_map/ppermute | solution.py:269
  25.4 3.4 %collective-permute-start.3 = (f32[80,256]{1,0:T(8,128)S(1)}, f32[80,256]{1,0:T(8,128)S(1)}, u32[]{:S(2)}, u32[]{:S(2)}) collective-permute-start(f32[80,256]{1,0:T(8,128)S(1)} %add.26), channel_id=1, source_target_pairs={{0,8},{8,0},{16,24},{24,16},{1,9},{9,1},{17,25},{25,17},{2,10},{10... | collective-permute-start | bytes 245768 | tf_op jit(solution)/shard_map/ppermute | solution.py:269
  28.8 4.6 %collective-permute-start.4 = (f32[80,256]{1,0:T(8,128)S(1)}, f32[80,256]{1,0:T(8,128)S(1)}, u32[]{:S(2)}, u32[]{:S(2)}) collective-permute-start(f32[80,256]{1,0:T(8,128)S(1)} %add.27), channel_id=1, source_target_pairs={{8,16},{16,8},{24,0},{0,24},{9,17},{17,9},{25,1},{1,25},{10,18},{1... | collective-permute-start | bytes 245768 | tf_op jit(solution)/shard_map/ppermute | solution.py:269
  33.4 3.7 %collective-permute-start.5 = (f32[80,256]{1,0:T(8,128)S(1)}, f32[80,256]{1,0:T(8,128)S(1)}, u32[]{:S(2)}, u32[]{:S(2)}) collective-permute-start(f32[80,256]{1,0:T(8,128)S(1)} %add.28), channel_id=1, source_target_pairs={{0,1},{1,0},{2,3},{3,2},{4,5},{5,4},{6,7},{7,6},{8,9},{9,8},{10,11... | collective-permute-start | bytes 245768 | tf_op jit(solution)/shard_map/ppermute | solution.py:269
  37.1 5.8 %collective-permute-start.6 = (f32[80,256]{1,0:T(8,128)S(1)}, f32[80,256]{1,0:T(8,128)S(1)}, u32[]{:S(2)}, u32[]{:S(2)}) collective-permute-start(f32[80,256]{1,0:T(8,128)S(1)} %add.29), channel_id=1, source_target_pairs={{1,2},{2,1},{3,4},{4,3},{5,6},{6,5},{7,0},{0,7},{9,10},{10,9},{11,... | collective-permute-start | bytes 245768 | tf_op jit(solution)/shard_map/ppermute | solution.py:269
  42.9 6.0 %collective-permute-start.7 = (f32[80,256]{1,0:T(8,128)S(1)}, f32[80,256]{1,0:T(8,128)S(1)}, u32[]{:S(2)}, u32[]{:S(2)}) collective-permute-start(f32[80,256]{1,0:T(8,128)S(1)} %add.30), channel_id=1, source_target_pairs={{0,3},{3,0},{1,6},{6,1},{2,5},{5,2},{4,7},{7,4},{8,11},{11,8},{9,1... | collective-permute-start | bytes 245768 | tf_op jit(solution)/shard_map/ppermute | solution.py:269
  49.0 7.8 %collective-permute-start.8 = (f32[80,256]{1,0:T(8,128)S(1)}, f32[80,256]{1,0:T(8,128)S(1)}, u32[]{:S(2)}, u32[]{:S(2)}) collective-permute-start(f32[80,256]{1,0:T(8,128)S(1)} %add.31), channel_id=1, source_target_pairs={{0,32},{32,0},{1,33},{33,1},{2,34},{34,2},{3,35},{35,3},{4,36},{36... | collective-permute-start | bytes 245768 | tf_op jit(solution)/shard_map/ppermute | solution.py:269

commit v4 on v3

--- a/solution.py
+++ b/solution.py
@@ -110,7 +110,6 @@
     b1, b2, b3 = cut(upper_inverse(prior_ref, small), 3)
     right = jnp.concatenate([b1, b2, b3, b1, b2, b1], axis=0)
     writes = []
-    sums = None
     for b, at in enumerate(blocks):
         a1, a2, a3 = (parts_ref[at, i * N : (i + 1) * N] for i in range(3))
         high, low = cut(dot(jnp.concatenate([a3, a2, a1, a2, a1, a1], axis=1), right), 2)
@@ -119,8 +118,7 @@
         for i, (source, target) in enumerate(((high_ref, high_out), (low_ref, low_out))):
             writes.append(pltpu.make_async_copy(source.at[at, :], target.at[at, :], out_sems.at[2 * b + i]))
             writes[-1].start()
-        gain = dot(high.T, jnp.concatenate([high, low], axis=1))
-        sums = gain if sums is None else sums + gain
+    sums = dot(high_ref[...], jnp.concatenate([high_ref[...], low_ref[...]], axis=1), ((0,), (0,)))
     mixed = sums[:, N:]
     gram = sums[:, :N] + (mixed + mixed.T)
     packed_ref[0:64, :] = gram[0:64, :]

time: 64.9 us -> 64.8 us (level)
  no operation moved by 1% of the time
where the time goes in v4:
time: 64.8 us; the launch traced here: 64.6 us
  waiting for transfers between devices  25.8 us (40%)
  Pallas kernels  18.2 us (28%)
  starting transfers between devices  18.1 us (28%)
  between operations  1.53 us (2%)
  local copies, waits for them, and re-layouts  0.94 us (1%)
    ppermute x9, waiting for transfers between devices, swap(): lax.ppermute(value, axis, [p for a, b in pairs for p in ((a, b), (b, a))])  25.8 us
    ppermute x9, starting transfers between devices, swap(): lax.ppermute(value, axis, [p for a, b in pairs for p in ((a, b), (b, a))])  18.1 us
    pallas_call x1, Pallas kernels, stage_one(): pl.pallas_call(first_kernel, out_shape=(jax.ShapeDtypeStruct((rows, N), B...  10.4 us
    pallas_call x1, Pallas kernels, stage_two(): pl.pallas_call(functools.partial(second_kernel, row_scale), out_shape=(ja...  7.78 us
  transfers between devices with their start and end apart: 9, of which 9 were waited for; matrix products, arithmetic and copies ran while one was open for 0% of the time, Pallas kernels for 0%

profile of v4, /device:TPU:1, one launch (start us, length us, event | category | flops | bytes accessed | tf_op | source)
XLA Modules:
  0.0 64.6 jit_solution(4220569338496304937)
XLA Ops:
  1.3 0.0 copy-start
  1.3 0.9 %copy-done = f32[256,256]{1,0:T(8,128)S(1)} copy-done((f32[256,256]{1,0:T(8,128)S(1)}, f32[256,256]{1,0:T(8,128)}, u32[]{:S(2)}) %copy-start) | copy-done | bytes 262168
  2.2 10.4 %shard_map.50 = (bf16[2048,256]{1,0:T(8,128)(2,1)S(1)}, bf16[2048,256]{1,0:T(8,128)(2,1)S(1)}, f32[160,256]{1,0:T(8,128)S(1)}) custom-call(s32[1]{0:T(128)S(6)} %copy.5.counts_ref, f32[2048,256]{1,0:T(8,128)} %span_ref.1, f32[256,256]{1,0:T(8,128)S(1)} %copy-done), custom_call_target="tpu_custom_call" | custom-call | tf_op jit(solution)/shard_map/pallas_call | solution.py:295
  12.7 3.3 %collective-permute-start = (f32[80,256]{1,0:T(8,128)S(1)}, f32[80,256]{1,0:T(8,128)S(1)}, u32[]{:S(2)}, u32[]{:S(2)}) collective-permute-start(f32[80,256]{1,0:T(8,128)S(1)} %slice_select_fusion), channel_id=1, source_target_pairs={{0,32},{32,0},{1,33},{33,1},{2,34},{34,2},{3,35},{35,3},{4,36},{36... | collective-permute-start | bytes 245768 | tf_op jit(solution)/shard_map/ppermute | solution.py:267
  16.0 0.9 %collective-permute-done = f32[80,256]{1,0:T(8,128)S(1)} collective-permute-done((f32[80,256]{1,0:T(8,128)S(1)}, f32[80,256]{1,0:T(8,128)S(1)}, u32[]{:S(2)}, u32[]{:S(2)}) %collective-permute-start) | collective-permute-done | bytes 81952 | tf_op jit(solution)/shard_map/ppermute | solution.py:267
  16.9 0.1 collective-permute-start.1
  17.0 3.7 %collective-permute-done.1 = f32[80,256]{1,0:T(8,128)S(1)} collective-permute-done((f32[80,256]{1,0:T(8,128)S(1)}, f32[80,256]{1,0:T(8,128)S(1)}, u32[]{:S(2)}, u32[]{:S(2)}) %collective-permute-start.1) | collective-permute-done | bytes 81952 | tf_op jit(solution)/shard_map/ppermute | solution.py:267
  20.7 0.8 %collective-permute-start.2 = (f32[80,256]{1,0:T(8,128)S(1)}, f32[80,256]{1,0:T(8,128)S(1)}, u32[]{:S(2)}, u32[]{:S(2)}) collective-permute-start(f32[80,256]{1,0:T(8,128)S(1)} %add.25), channel_id=1, source_target_pairs={{64,128},{128,64},{192,0},{0,192},{65,129},{129,65},{193,1},{1,193... | collective-permute-start | bytes 245768 | tf_op jit(solution)/shard_map/ppermute | solution.py:267
  21.5 3.8 %collective-permute-done.2 = f32[80,256]{1,0:T(8,128)S(1)} collective-permute-done((f32[80,256]{1,0:T(8,128)S(1)}, f32[80,256]{1,0:T(8,128)S(1)}, u32[]{:S(2)}, u32[]{:S(2)}) %collective-permute-start.2) | collective-permute-done | bytes 81952 | tf_op jit(solution)/shard_map/ppermute | solution.py:267
  25.3 0.1 collective-permute-start.3
  25.4 3.3 %collective-permute-done.3 = f32[80,256]{1,0:T(8,128)S(1)} collective-permute-done((f32[80,256]{1,0:T(8,128)S(1)}, f32[80,256]{1,0:T(8,128)S(1)}, u32[]{:S(2)}, u32[]{:S(2)}) %collective-permute-start.3) | collective-permute-done | bytes 81952 | tf_op jit(solution)/shard_map/ppermute | solution.py:267
  28.7 1.1 %collective-permute-start.4 = (f32[80,256]{1,0:T(8,128)S(1)}, f32[80,256]{1,0:T(8,128)S(1)}, u32[]{:S(2)}, u32[]{:S(2)}) collective-permute-start(f32[80,256]{1,0:T(8,128)S(1)} %add.27), channel_id=1, source_target_pairs={{8,16},{16,8},{24,0},{0,24},{9,17},{17,9},{25,1},{1,25},{10,18},{1... | collective-permute-start | bytes 245768 | tf_op jit(solution)/shard_map/ppermute | solution.py:267
  29.8 3.5 %collective-permute-done.4 = f32[80,256]{1,0:T(8,128)S(1)} collective-permute-done((f32[80,256]{1,0:T(8,128)S(1)}, f32[80,256]{1,0:T(8,128)S(1)}, u32[]{:S(2)}, u32[]{:S(2)}) %collective-permute-start.4) | collective-permute-done | bytes 81952 | tf_op jit(solution)/shard_map/ppermute | solution.py:267
  33.3 0.1 collective-permute-start.5
  33.4 3.6 %collective-permute-done.5 = f32[80,256]{1,0:T(8,128)S(1)} collective-permute-done((f32[80,256]{1,0:T(8,128)S(1)}, f32[80,256]{1,0:T(8,128)S(1)}, u32[]{:S(2)}, u32[]{:S(2)}) %collective-permute-start.5) | collective-permute-done | bytes 81952 | tf_op jit(solution)/shard_map/ppermute | solution.py:267
  37.0 4.0 %collective-permute-start.6 = (f32[80,256]{1,0:T(8,128)S(1)}, f32[80,256]{1,0:T(8,128)S(1)}, u32[]{:S(2)}, u32[]{:S(2)}) collective-permute-start(f32[80,256]{1,0:T(8,128)S(1)} %add.29), channel_id=1, source_target_pairs={{1,2},{2,1},{3,4},{4,3},{5,6},{6,5},{7,0},{0,7},{9,10},{10,9},{11,... | collective-permute-start | bytes 245768 | tf_op jit(solution)/shard_map/ppermute | solution.py:267
  41.0 1.8 %collective-permute-done.6 = f32[80,256]{1,0:T(8,128)S(1)} collective-permute-done((f32[80,256]{1,0:T(8,128)S(1)}, f32[80,256]{1,0:T(8,128)S(1)}, u32[]{:S(2)}, u32[]{:S(2)}) %collective-permute-start.6) | collective-permute-done | bytes 81952 | tf_op jit(solution)/shard_map/ppermute | solution.py:267
  42.8 1.7 %collective-permute-start.7 = (f32[80,256]{1,0:T(8,128)S(1)}, f32[80,256]{1,0:T(8,128)S(1)}, u32[]{:S(2)}, u32[]{:S(2)}) collective-permute-start(f32[80,256]{1,0:T(8,128)S(1)} %add.30), channel_id=1, source_target_pairs={{0,3},{3,0},{1,6},{6,1},{2,5},{5,2},{4,7},{7,4},{8,11},{11,8},{9,1... | collective-permute-start | bytes 245768 | tf_op jit(solution)/shard_map/ppermute | solution.py:267
  44.5 4.3 %collective-permute-done.7 = f32[80,256]{1,0:T(8,128)S(1)} collective-permute-done((f32[80,256]{1,0:T(8,128)S(1)}, f32[80,256]{1,0:T(8,128)S(1)}, u32[]{:S(2)}, u32[]{:S(2)}) %collective-permute-start.7) | collective-permute-done | bytes 81952 | tf_op jit(solution)/shard_map/ppermute | solution.py:267
  48.9 6.8 %collective-permute-start.8 = (f32[80,256]{1,0:T(8,128)S(1)}, f32[80,256]{1,0:T(8,128)S(1)}, u32[]{:S(2)}, u32[]{:S(2)}) collective-permute-start(f32[80,256]{1,0:T(8,128)S(1)} %add.31), channel_id=1, source_target_pairs={{0,32},{32,0},{1,33},{33,1},{2,34},{34,2},{3,35},{35,3},{4,36},{36... | collective-permute-start | bytes 245768 | tf_op jit(solution)/shard_map/ppermute | solution.py:267
  55.7 0.9 %collective-permute-done.8 = f32[80,256]{1,0:T(8,128)S(1)} collective-permute-done((f32[80,256]{1,0:T(8,128)S(1)}, f32[80,256]{1,0:T(8,128)S(1)}, u32[]{:S(2)}, u32[]{:S(2)}) %collective-permute-start.8) | collective-permute-done | bytes 81952 | tf_op jit(solution)/shard_map/ppermute | solution.py:267
  56.7 7.8 %shard_map.51 = (f32[256,256]{1,0:T(8,128)}, f32[2048,256]{1,0:T(8,128)}) custom-call(f32[160,256]{1,0:T(8,128)S(1)} %pad_maximum_fusion.packed_ref, f32[256,256]{1,0:T(8,128)S(1)} %copy-done, bf16[2048,256]{1,0:T(8,128)(2,1)S(1)} %get-tuple-element.6.high_ref, bf16[2048,256]{1,0:T(8,128)(2,1)S(1)} %get-tuple-element.7.low_ref), custom_call_target="tpu_custom_call" | custom-call | tf_op jit(solution)/shard_map/pallas_call | solution.py:318
  (11 shorter events, 0.1 us)
Async XLA Ops:
  1.3 1.0 %copy-start = (f32[256,256]{1,0:T(8,128)S(1)}, f32[256,256]{1,0:T(8,128)}, u32[]{:S(2)}) copy-start(f32[256,256]{1,0:T(8,128)} %prior_ref.3) | copy-start | bytes 786436
  12.7 4.3 %collective-permute-start = (f32[80,256]{1,0:T(8,128)S(1)}, f32[80,256]{1,0:T(8,128)S(1)}, u32[]{:S(2)}, u32[]{:S(2)}) collective-permute-start(f32[80,256]{1,0:T(8,128)S(1)} %slice_select_fusion), channel_id=1, source_target_pairs={{0,32},{32,0},{1,33},{33,1},{2,34},{34,2},{3,35},{35,3},{4,36},{36... | collective-permute-start | bytes 245768 | tf_op jit(solution)/shard_map/ppermute | solution.py:267
  16.9 3.8 %collective-permute-start.1 = (f32[80,256]{1,0:T(8,128)S(1)}, f32[80,256]{1,0:T(8,128)S(1)}, u32[]{:S(2)}, u32[]{:S(2)}) collective-permute-start(f32[80,256]{1,0:T(8,128)S(1)} %select_add_fusion), channel_id=1, source_target_pairs={{0,64},{64,0},{128,192},{192,128},{1,65},{65,1},{129,193},{193,129... | collective-permute-start | bytes 245768 | tf_op jit(solution)/shard_map/ppermute | solution.py:267
  20.7 4.6 %collective-permute-start.2 = (f32[80,256]{1,0:T(8,128)S(1)}, f32[80,256]{1,0:T(8,128)S(1)}, u32[]{:S(2)}, u32[]{:S(2)}) collective-permute-start(f32[80,256]{1,0:T(8,128)S(1)} %add.25), channel_id=1, source_target_pairs={{64,128},{128,64},{192,0},{0,192},{65,129},{129,65},{193,1},{1,193... | collective-permute-start | bytes 245768 | tf_op jit(solution)/shard_map/ppermute | solution.py:267
  25.3 3.4 %collective-permute-start.3 = (f32[80,256]{1,0:T(8,128)S(1)}, f32[80,256]{1,0:T(8,128)S(1)}, u32[]{:S(2)}, u32[]{:S(2)}) collective-permute-start(f32[80,256]{1,0:T(8,128)S(1)} %add.26), channel_id=1, source_target_pairs={{0,8},{8,0},{16,24},{24,16},{1,9},{9,1},{17,25},{25,17},{2,10},{10... | collective-permute-start | bytes 245768 | tf_op jit(solution)/shard_map/ppermute | solution.py:267
  28.7 4.6 %collective-permute-start.4 = (f32[80,256]{1,0:T(8,128)S(1)}, f32[80,256]{1,0:T(8,128)S(1)}, u32[]{:S(2)}, u32[]{:S(2)}) collective-permute-start(f32[80,256]{1,0:T(8,128)S(1)} %add.27), channel_id=1, source_target_pairs={{8,16},{16,8},{24,0},{0,24},{9,17},{17,9},{25,1},{1,25},{10,18},{1... | collective-permute-start | bytes 245768 | tf_op jit(solution)/shard_map/ppermute | solution.py:267
  33.3 3.7 %collective-permute-start.5 = (f32[80,256]{1,0:T(8,128)S(1)}, f32[80,256]{1,0:T(8,128)S(1)}, u32[]{:S(2)}, u32[]{:S(2)}) collective-permute-start(f32[80,256]{1,0:T(8,128)S(1)} %add.28), channel_id=1, source_target_pairs={{0,1},{1,0},{2,3},{3,2},{4,5},{5,4},{6,7},{7,6},{8,9},{9,8},{10,11... | collective-permute-start | bytes 245768 | tf_op jit(solution)/shard_map/ppermute | solution.py:267
  37.0 5.8 %collective-permute-start.6 = (f32[80,256]{1,0:T(8,128)S(1)}, f32[80,256]{1,0:T(8,128)S(1)}, u32[]{:S(2)}, u32[]{:S(2)}) collective-permute-start(f32[80,256]{1,0:T(8,128)S(1)} %add.29), channel_id=1, source_target_pairs={{1,2},{2,1},{3,4},{4,3},{5,6},{6,5},{7,0},{0,7},{9,10},{10,9},{11,... | collective-permute-start | bytes 245768 | tf_op jit(solution)/shard_map/ppermute | solution.py:267
  42.8 6.0 %collective-permute-start.7 = (f32[80,256]{1,0:T(8,128)S(1)}, f32[80,256]{1,0:T(8,128)S(1)}, u32[]{:S(2)}, u32[]{:S(2)}) collective-permute-start(f32[80,256]{1,0:T(8,128)S(1)} %add.30), channel_id=1, source_target_pairs={{0,3},{3,0},{1,6},{6,1},{2,5},{5,2},{4,7},{7,4},{8,11},{11,8},{9,1... | collective-permute-start | bytes 245768 | tf_op jit(solution)/shard_map/ppermute | solution.py:267
  48.9 7.8 %collective-permute-start.8 = (f32[80,256]{1,0:T(8,128)S(1)}, f32[80,256]{1,0:T(8,128)S(1)}, u32[]{:S(2)}, u32[]{:S(2)}) collective-permute-start(f32[80,256]{1,0:T(8,128)S(1)} %add.31), channel_id=1, source_target_pairs={{0,32},{32,0},{1,33},{33,1},{2,34},{34,2},{3,35},{35,3},{4,36},{36... | collective-permute-start | bytes 245768 | tf_op jit(solution)/shard_map/ppermute | solution.py:267
